TPU v7x, 128 devices: a whole 4x4x4 slice. The times are simulated.
128 devices in a mesh: dom: 64 (over x, z, y), rhs: 2 (over core).
Axes of the slice: x: 4, y: 4, z: 4, core: 2. Of those that a mesh axis runs over, the one named last changes fastest.
Arguments:
- adjoint: bfloat16 [1024, 64, 320], P('dom', 'rhs'), may hold values from -6 to 6
- adj_rhs: float32 [1024, 64, 320], P('dom', 'rhs'), may hold values from -6 to 6
- diag_inv: bfloat16 [1024, 320, 320], P('dom'), may hold values from -0.3125 to 0.3125
- diag_jac: bfloat16 [1024, 320, 320], P('dom'), may hold values from -0.3125 to 0.3125
- upper: bfloat16 [1024, 4, 320, 320], P('dom', 'rhs'), may hold values from -0.25 to 0.25
- face_jac: bfloat16 [1024, 4, 320, 320], P('dom', 'rhs'), may hold values from -0.25 to 0.25
- face_ref: int32 [1024, 4], P('dom'), may hold values from 0 to 79, as said below
- send_list: int32 [64, 64, 1], P('dom'), may hold values from 0 to 15
- colour: int32 [1024], P('dom'), may hold values from 0 to 3, as said below
Outputs:
- adjoint_new: bfloat16 [1024, 64, 320], P('dom', 'rhs')
- residual: float32 [1024, 64, 320], P('dom', 'rhs')
Inputs may be any that keep to these rules, and one draw needn't show every extreme that they name: `face_ref`: for an element of partition d, a value below 16 names another of d's own elements; a value 16 + 1 * q + s with 0 <= s < 1 names the element that partition q lists in send_list[q, d, s]. Each partition reads from exactly 32 other partitions, and each of their 1 slots is named by exactly one face of the partition; other slots are never named. Each partition has between 1 and 8 elements of colour 0, and some partition has exactly 8.
All inputs are finite; a program needn't handle non-finite values.
Results may differ from a plain program's by a relative error of at most 0.0034.
Values may be sent and summed in bfloat16 or wider, within the bound.
No kernel may reach another device: no remote copies, remote signals or barrier semaphores. Data moves between devices by JAX's collectives and lax.ppermute only.
A program may use at most 128 MiB of HBM per device.

v0:
```python
import jax
import jax.numpy as jnp
from jax import lax
from jax.sharding import PartitionSpec as P


def on_device(adjoint, adj_rhs, diag_inv, diag_jac, upper, face_jac, face_ref, send_list, colour):
    part_count = lax.axis_size("dom")
    elem_count, width_r, width_n = adjoint.shape
    send_table = send_list[0]
    slot_count = send_table.shape[1]
    outgoing = adjoint[send_table]
    incoming = lax.all_to_all(outgoing, "dom", split_axis=0, concat_axis=0, tiled=True)
    extended = jnp.concatenate(
        [adjoint, incoming.reshape((part_count * slot_count, width_r, width_n))], 0
    )
    neighbours = extended[face_ref]
    pushed = jnp.einsum(
        "efrn,efnm->erm",
        neighbours,
        lax.all_gather(upper, "rhs", axis=1, tiled=True),
        preferred_element_type=jnp.float32,
    )
    reduced = (adj_rhs - pushed).astype(jnp.bfloat16)
    swept_rows = jnp.einsum(
        "ern,enm->erm", reduced, diag_inv, preferred_element_type=jnp.float32
    ).astype(jnp.bfloat16)
    kept_rows = jnp.where((colour == 0)[:, None, None], swept_rows, adjoint)
    ext_rows = elem_count + part_count * slot_count
    segment = lax.all_gather(face_jac, "rhs", axis=1, tiled=True)
    face_count = segment.shape[1]
    partial_value = jnp.einsum(
        "ern,efnm->efrm", kept_rows, segment, preferred_element_type=jnp.float32
    )
    face_rows = face_ref.reshape(-1)
    gathered = jax.ops.segment_sum(
        partial_value.reshape((elem_count * face_count, width_r, width_n)),
        face_rows,
        num_segments=ext_rows,
    )
    outbound = (
        gathered[elem_count:]
        .astype(jnp.bfloat16)
        .reshape((part_count, slot_count, width_r, width_n))
    )
    inbound = lax.all_to_all(outbound, "dom", split_axis=0, concat_axis=0, tiled=True)
    returned = jax.ops.segment_sum(
        inbound.reshape((part_count * slot_count, width_r, width_n)).astype(jnp.float32),
        send_table.reshape(-1),
        num_segments=elem_count,
    )
    applied = (
        jnp.einsum("ern,enm->erm", kept_rows, diag_jac, preferred_element_type=jnp.float32)
        + gathered[:elem_count]
        + returned
    )
    return (kept_rows, adj_rhs - applied)


def solution(mesh):
    in_specs = (
        P("dom", "rhs", None),
        P("dom", "rhs", None),
        P("dom", None, None),
        P("dom", None, None),
        P("dom", "rhs", None, None),
        P("dom", "rhs", None, None),
        P("dom", None),
        P("dom", None, None),
        P("dom"),
    )
    out_specs = (P("dom", "rhs", None), P("dom", "rhs", None))
    return jax.shard_map(
        on_device, mesh=mesh, in_specs=in_specs, out_specs=out_specs, check_vma=False
    )
```

profile of v0, /device:TPU:0, one launch (start us, length us, event | category | flops | bytes accessed | tf_op | source)
XLA Modules:
  0.0 153.5 jit_solution(14713598401540233295)
XLA Ops:
  7.2 0.0 all-gather.3.cloned.1.call-start
  7.2 0.7 all-gather.3.cloned.1.call-update
  7.9 0.0 copy-start.6
  7.9 0.0 copy-start
  7.9 0.0 all-gather.5.cloned.1.call-start
  8.0 0.7 all-gather.5.cloned.1.call-update
  8.7 0.0 copy-done.6
  8.7 0.2 copy-done
  8.9 0.0 copy-start.5
  8.9 0.0 copy-start.7
  8.9 1.9 %gather_fusion = bf16[64,32,320]{2,1,0:T(8,128)(2,1)} fusion(bf16[16,32,320]{2,1,0:T(8,128)(2,1)S(1)} %copy-done, s32[1024]{0:T(1024)S(1)} %pad_clamp_fusion.1), kind=kCustom, calls=%fused_computation | custom fusion | bytes 2621696 | tf_op jit(solution)/shard_map/gather | solution.py:12
  10.8 11.5 %all-to-all-start = ((bf16[64,1,32,320]{3,2,1,0:T(8,128)(2,1)}), bf16[64,1,32,320]{3,2,1,0:T(8,128)(2,1)S(1)}, u32[]{:S(2)}, u32[]{:S(2)}) async-start(bf16[64,1,32,320]{3,2,1,0:T(8,128)(2,1)} %bitcast.2), calls=%async_computation | async-start | bytes 3145728 | tf_op jit(solution)/shard_map/all_to_all | solution.py:13
  22.3 0.0 copy-done.5
  22.4 0.1 copy.16
  22.4 0.1 copy.15
  22.5 0.1 reshape.70
  22.6 0.1 reshape.78
  22.7 0.0 copy-done.7
  22.7 23.8 %all-to-all-done = bf16[64,1,32,320]{3,2,1,0:T(8,128)(2,1)S(1)} async-done(((bf16[64,1,32,320]{3,2,1,0:T(8,128)(2,1)}), bf16[64,1,32,320]{3,2,1,0:T(8,128)(2,1)S(1)}, u32[]{:S(2)}, u32[]{:S(2)}) %all-to-all-start) | async-done | bytes 1310752 | tf_op jit(solution)/shard_map/all_to_all | solution.py:13
  46.5 0.0 copy-start.1
  46.5 1.2 copy-done.1
  47.7 0.0 copy-start.3
  47.7 1.8 %pad_maximum_fusion = bf16[80,32,320]{2,1,0:T(8,128)(2,1)S(1)} fusion(bf16[64,32,320]{2,1,0:T(8,128)(2,1)} %bitcast.42, bf16[16,32,320]{2,1,0:T(8,128)(2,1)S(1)} %copy-done), kind=kLoop, calls=%fused_computation.5 | loop fusion | flops 819200 | bytes 3276800 | tf_op jit(solution)/shard_map/concatenate | solution.py:14
  49.5 1.9 %gather_fusion.1 = bf16[64,32,320]{2,1,0:T(8,128)(2,1)} fusion(bf16[80,32,320]{2,1,0:T(8,128)(2,1)S(1)} %pad_maximum_fusion, s32[1024]{0:T(1024)S(1)} %pad_clamp_fusion), kind=kCustom, calls=%fused_computation.1 | custom fusion | bytes 2621696 | tf_op jit(solution)/shard_map/gather | solution.py:17
  51.4 0.0 all-gather.3.cloned.1.call-done
  51.4 0.0 copy-done.3
  51.4 13.1 %fusion.3 = bf16[16,32,320]{2,1,0:T(8,128)(2,1)S(1)} fusion(bf16[16,32,320]{2,1,0:T(8,128)(2,1)S(1)} %copy-done, bf16[16,320,320]{2,1,0:T(8,128)(2,1)} %param.11, f32[16,32,320]{2,1,0:T(8,128)S(1)} %copy-done.3, bf16[16,4,32,320]{3,2,1,0:T(8,128)(2,1)} %bitcast.41, bf16[16,4,320,320]{3,2,1,0:T(8,128)(2,1)} %all-gather.3.cloned.1.call-done, ...), kind=kOutput, calls=%fused_computation.13 | convolution fusion | flops 524943360 | bytes 19005456 | tf_op jit(solution)/shard_map/ern,enm->erm/dot_general | solution.py:25
  64.5 0.0 copy-start.2
  64.5 13.4 %all-gather.5.cloned.1.call-done = bf16[16,4,320,320]{3,2,1,0:T(8,128)(2,1)} async-done(((bf16[16,2,320,320]{3,2,1,0:T(8,128)(2,1)}), bf16[16,4,320,320]{3,2,1,0:T(8,128)(2,1)}) %all-gather.5.cloned.1.call-update) | async-done | bytes 13107216 | tf_op jit(solution)/shard_map/all_gather | solution.py:30
  77.9 6.9 %fusion.4 = f32[16,32,4,320]{3,1,2,0:T(8,128)S(1)} fusion(bf16[16,4,320,320]{3,2,1,0:T(8,128)(2,1)} %all-gather.5.cloned.1.call-done, bf16[16,32,320]{2,1,0:T(8,128)(2,1)S(1)} %fusion.3), kind=kOutput, calls=%fused_computation.14 | convolution fusion | flops 419430400 | bytes 16056320 | tf_op jit(solution)/shard_map/ern,efnm->efrm/dot_general | solution.py:32
  84.8 2.4 %broadcast_in_dim.19 = f32[80,32,320]{2,1,0:T(8,128)} broadcast(f32[]{:T(128)} %constant.0.clone.1), dimensions={} | broadcast | bytes 3276804 | tf_op jit(solution)/shard_map/broadcast_in_dim | solution.py:36
  87.1 10.3 %scatter_fusion = f32[80,32,320]{2,1,0:T(8,128)} fusion(f32[80,32,320]{2,1,0:T(8,128)} %broadcast_in_dim.19, s32[64]{0:T(128)S(1)} %reshape.78, f32[64,32,320]{2,1,0:T(8,128)S(1)} %bitcast.40), kind=kCustom, calls=%fused_computation.2 | custom fusion | flops 655360 | bytes 7864576 | tf_op jit(solution)/shard_map/scatter-add | solution.py:36
  97.5 3.3 %fusion = bf16[64,1,32,320]{3,2,1,0:T(8,128)(2,1)} fusion(f32[80,32,320]{2,1,0:T(8,128)} %scatter_fusion), kind=kLoop, calls=%fused_computation.6 | loop fusion | bytes 2621440 | tf_op jit(solution)/shard_map/reshape | solution.py:44
  100.7 10.3 %all-to-all-start.1 = ((bf16[64,1,32,320]{3,2,1,0:T(8,128)(2,1)}), bf16[64,1,32,320]{3,2,1,0:T(8,128)(2,1)S(1)}, u32[]{:S(2)}, u32[]{:S(2)}) async-start(bf16[64,1,32,320]{3,2,1,0:T(8,128)(2,1)} %fusion), calls=%async_computation.1 | async-start | bytes 3145728 | tf_op jit(solution)/shard_map/all_to_all | solution.py:46
  111.1 0.0 copy-done.2
  111.1 3.0 %convolution_add_fusion = f32[16,32,320]{2,1,0:T(8,128)S(1)} fusion(bf16[16,32,320]{2,1,0:T(8,128)(2,1)S(1)} %fusion.3, bf16[16,320,320]{2,1,0:T(8,128)(2,1)} %param.12, f32[80,32,320]{2,1,0:T(8,128)} %scatter_fusion), kind=kOutput, calls=%fused_computation.10 | convolution fusion | flops 105021440 | bytes 4915200 | tf_op jit(solution)/shard_map/ern,enm->erm/dot_general | solution.py:53
  114.1 21.6 %all-to-all-done.1 = bf16[64,1,32,320]{3,2,1,0:T(8,128)(2,1)S(1)} async-done(((bf16[64,1,32,320]{3,2,1,0:T(8,128)(2,1)}), bf16[64,1,32,320]{3,2,1,0:T(8,128)(2,1)S(1)}, u32[]{:S(2)}, u32[]{:S(2)}) %all-to-all-start.1) | async-done | bytes 1310752 | tf_op jit(solution)/shard_map/all_to_all | solution.py:46
  135.7 2.0 %bitcast_convert_fusion = f32[64,32,320]{2,1,0:T(8,128)} fusion(bf16[64,1,32,320]{3,2,1,0:T(8,128)(2,1)S(1)} %all-to-all-done.1), kind=kLoop, calls=%fused_computation.7 | loop fusion | flops 655360 | bytes 3932160 | tf_op jit(solution)/shard_map/convert_element_type | solution.py:48
  137.7 0.0 copy-start.4
  137.7 8.0 %scatter_fusion.1 = f32[16,32,320]{2,1,0:T(8,128)S(1)} fusion(f32[16,32,320]{2,1,0:T(8,128)S(1)} %convolution_add_fusion, s32[64]{0:T(128)S(1)} %bitcast.43, f32[64,32,320]{2,1,0:T(8,128)} %bitcast_convert_fusion), kind=kCustom, calls=%fused_computation.3 | custom fusion | flops 655360 | bytes 7864576 | tf_op jit(solution)/shard_map/scatter-add | solution.py:47
  145.7 0.0 copy-done.4
  145.7 1.0 sub.7
  (5 shorter events, 0.0 us)
Async XLA Ops:
  7.2 44.3 %all-gather.3.cloned.1.call-start = ((), (), s32[]{:S(2)}) async-start(), calls=%async_computation.2 | async-start | bytes 23592960 | tf_op jit(solution)/shard_map/all_gather | solution.py:21
  7.9 0.8 copy-start.6
  7.9 1.0 copy-start
  7.9 70.0 %all-gather.5.cloned.1.call-start = ((), (), s32[]{:S(2)}) async-start(), calls=%async_computation.3 | async-start | bytes 23592960 | tf_op jit(solution)/shard_map/all_gather | solution.py:30
  8.9 13.4 %copy-start.5 = (s32[16,4]{0,1:T(4,128)S(1)}, s32[16,4]{0,1:T(4,128)}, u32[]{:S(2)}) copy-start(s32[16,4]{0,1:T(4,128)} %param.15) | copy-start | bytes 772
  8.9 13.8 %copy-start.7 = (s32[16]{0:T(128)S(1)}, s32[16]{0:T(128)}, u32[]{:S(2)}) copy-start(s32[16]{0:T(128)} %param.17) | copy-start | bytes 196
  10.8 35.7 %all-to-all-start = ((bf16[64,1,32,320]{3,2,1,0:T(8,128)(2,1)}), bf16[64,1,32,320]{3,2,1,0:T(8,128)(2,1)S(1)}, u32[]{:S(2)}, u32[]{:S(2)}) async-start(bf16[64,1,32,320]{3,2,1,0:T(8,128)(2,1)} %bitcast.2), calls=%async_computation | async-start | bytes 3145728 | tf_op jit(solution)/shard_map/all_to_all | solution.py:13
  46.5 1.2 copy-start.1
  47.7 3.8 %copy-start.3 = (f32[16,32,320]{2,1,0:T(8,128)S(1)}, f32[16,32,320]{2,1,0:T(8,128)}, u32[]{:S(2)}) copy-start(f32[16,32,320]{2,1,0:T(8,128)} %param.10) | copy-start | bytes 1966084
  64.5 46.5 %copy-start.2 = (bf16[16,32,320]{2,1,0:T(8,128)(2,1)}, bf16[16,32,320]{2,1,0:T(8,128)(2,1)S(1)}, u32[]{:S(2)}) copy-start(bf16[16,32,320]{2,1,0:T(8,128)(2,1)S(1)} %fusion.3) | copy-start | bytes 983044
  100.7 34.9 %all-to-all-start.1 = ((bf16[64,1,32,320]{3,2,1,0:T(8,128)(2,1)}), bf16[64,1,32,320]{3,2,1,0:T(8,128)(2,1)S(1)}, u32[]{:S(2)}, u32[]{:S(2)}) async-start(bf16[64,1,32,320]{3,2,1,0:T(8,128)(2,1)} %fusion), calls=%async_computation.1 | async-start | bytes 3145728 | tf_op jit(solution)/shard_map/all_to_all | solution.py:46
  137.7 8.0 %copy-start.4 = (f32[16,32,320]{2,1,0:T(8,128)S(1)}, f32[16,32,320]{2,1,0:T(8,128)}, u32[]{:S(2)}) copy-start(f32[16,32,320]{2,1,0:T(8,128)} %param.10) | copy-start | bytes 1966084
Sparse Core Ops, SparseCore 0:
  9.7 33.7 all-gather.2
  45.2 32.6 all-gather.4
where the time goes:
time: 154 us
  waiting for transfers between devices  60.1 us (39%)
  other arithmetic  23.2 us (15%)
  matrix products  23 us (15%)
  starting transfers between devices  21.9 us (14%)
  between operations  14.2 us (9%)
  local copies, waits for them, and re-layouts  11.2 us (7%)
    all_to_all x1, waiting for transfers between devices, on_device(): lax.all_to_all(outgoing, 'dom', split_axis=0, concat_axis=0, tiled=True)  23.8 us
    all_to_all x1, waiting for transfers between devices, on_device(): lax.all_to_all(outbound, 'dom', split_axis=0, concat_axis=0, tiled=True)  21.6 us
    all_gather x1, waiting for transfers between devices, on_device(): segment = lax.all_gather(face_jac, 'rhs', axis=1, tiled=True)  13.4 us
    dot_general x1, matrix products, on_device(): jnp.einsum('ern,enm->erm', reduced, diag_inv, preferred_element_type=jnp....  13.1 us
    all_to_all x1, starting transfers between devices, on_device(): lax.all_to_all(outgoing, 'dom', split_axis=0, concat_axis=0, tiled=True)  11.5 us
    all_to_all x1, starting transfers between devices, on_device(): lax.all_to_all(outbound, 'dom', split_axis=0, concat_axis=0, tiled=True)  10.3 us
    scatter-add x1, other arithmetic, on_device(): jax.ops.segment_sum(partial_value.reshape((elem_count * face_count, width...  10.3 us
    scatter-add x1, other arithmetic, on_device(): jax.ops.segment_sum(inbound.reshape((part_count * slot_count, width_r, wi...  7.98 us
  transfers between devices with their start and end apart: 4, of which 3 were waited for; matrix products, arithmetic and copies ran while one was open for 14% of the time, Pallas kernels for 0%

commit v1 on v0

v1 whole, which is shorter than its diff:
```python
import jax
import jax.numpy as jnp
from jax import lax
from jax.experimental import pallas as pl
from jax.experimental.pallas import tpu as pltpu
from jax.sharding import PartitionSpec as P

N_EL, N_FACE, N_PART, C_MAX = 16, 4, 64, 8
R, N = 32, 320
MIB = 2**20

REF, SEND, COL, CORE = 0, 64, 128, 144

SMEM = pl.BlockSpec(memory_space=pltpu.SMEM)
VMEM = pl.BlockSpec(memory_space=pltpu.VMEM)
ANY = pl.BlockSpec(memory_space=pl.ANY)


def dot(a, b):
    return jnp.dot(a, b, preferred_element_type=jnp.float32)


def pack(v):
    tail = jnp.concatenate([v[:16, 256:], v[16:, 256:]], axis=1)
    return jnp.concatenate([v[:, :128], v[:, 128:256], tail], axis=0)


def unpack(p):
    tail = jnp.concatenate([p[64:, :64], p[64:, 64:]], axis=0)
    return jnp.concatenate([p[:32], p[32:64], tail], axis=1)


def order_by_colour(meta, order):
    def place(e, carry):
        zeros, others = carry
        is_zero = meta[COL + e] == 0
        order[jnp.where(is_zero, zeros, 15 - others)] = e
        step = is_zero.astype(jnp.int32)
        return zeros + step, others + 1 - step

    return lax.fori_loop(0, N_EL, place, (jnp.int32(0), jnp.int32(0)))[0]


def pack_kernel(meta, adj, out, packed):
    for e in range(N_EL):
        packed[e] = pack(adj[e])

    @pl.loop(0, N_PART, unroll=4)
    def _(q):
        out[q] = packed[meta[SEND + q]]


def select_kernel(meta, upper, out, order, sems):
    order_by_colour(meta, order)

    def copy(s):
        return pltpu.make_async_copy(upper.at[order[s]], out.at[s], sems.at[s])

    for s in range(C_MAX):
        copy(s).start()
    for s in range(C_MAX):
        copy(s).wait()


def face_copies(core, own_ref, own_at, other_ref, other_at, buf, slot, sem):
    own = pltpu.make_async_copy(
        own_ref.at[own_at], buf.at[slot, pl.ds(2 * core, 2)], sem.at[slot, 0]
    )
    other = pltpu.make_async_copy(
        other_ref.at[other_at], buf.at[slot, pl.ds(2 - 2 * core, 2)], sem.at[slot, 1]
    )
    return own, other


def faces_of(meta, e, x, weights, slot, send, local):
    for f in range(N_FACE):
        ref = meta[REF + e * N_FACE + f]
        product = dot(x, weights[slot, f])
        send[jnp.where(ref >= N_EL, ref - N_EL, N_PART)] = pack(product.astype(jnp.bfloat16))
        row = jnp.minimum(ref, N_EL)
        local[row] += product


def early_kernel(meta, adj, fj_own, fj_other, send_out, local_out, order, send, local, buf, sem):
    core = meta[CORE]
    count = order_by_colour(meta, order)

    def copies(s):
        e = order[s]
        return face_copies(core, fj_own, e, fj_other, e, buf, s, sem)

    @pl.loop(count, N_EL)
    def _(s):
        for c in copies(s):
            c.start()

    send[...] = jnp.zeros_like(send)
    local[...] = jnp.zeros_like(local)

    @pl.loop(count, N_EL)
    def _(s):
        for c in copies(s):
            c.wait()
        e = order[s]
        faces_of(meta, e, adj[e], buf, s, send, local)

    send_out[...] = send[:N_PART]
    local_out[...] = local[:N_EL]


def sweep_kernel(
    meta, adj, rhs, recv, send_in, local_in, upper, upper_other, dinv, fj_own, fj_other,
    new_out, send_out, local_out,
    order, send, local, red, new, up_buf, dinv_buf, fj_buf, up_sem, dinv_sem, fj_sem,
):
    core = meta[CORE]
    count = order_by_colour(meta, order)

    def up_copies(s):
        return face_copies(core, upper, order[s], upper_other, s, up_buf, s, up_sem)

    def dinv_copy(s):
        return pltpu.make_async_copy(dinv.at[order[s]], dinv_buf.at[s], dinv_sem.at[s])

    def fj_copies(s):
        return face_copies(core, fj_own, order[s], fj_other, order[s], fj_buf, s, fj_sem)

    @pl.loop(0, count)
    def _(s):
        for c in up_copies(s):
            c.start()

    @pl.loop(0, count)
    def _(s):
        dinv_copy(s).start()

    @pl.loop(0, count)
    def _(s):
        for c in fj_copies(s):
            c.start()

    new_out[...] = adj[...]
    send[:N_PART] = send_in[...]
    local[:N_EL] = local_in[...]
    local[N_EL] = jnp.zeros_like(local[N_EL])

    @pl.loop(0, count)
    def _(s):
        for c in up_copies(s):
            c.wait()
        e = order[s]
        total = jnp.zeros((R, N), jnp.float32)
        for f in range(N_FACE):
            ref = meta[REF + e * N_FACE + f]
            near = adj[jnp.minimum(ref, N_EL - 1)]
            far = unpack(recv[jnp.maximum(ref - N_EL, 0)])
            total += dot(jnp.where(ref < N_EL, near, far), up_buf[s, f])
        red[s] = (rhs[e] - total).astype(jnp.bfloat16)

    for half in range(2):

        @pl.when(count > 4 * half)
        def _():
            for s in range(4 * half, 4 * half + 4):

                @pl.when(s < count)
                def _():
                    dinv_copy(s).wait()

            for s in range(4 * half, 4 * half + 4):
                new[s] = dot(red[s], dinv_buf[s]).astype(jnp.bfloat16)

    @pl.loop(0, count)
    def _(s):
        for c in fj_copies(s):
            c.wait()
        e = order[s]
        new_out[e] = new[s]
        faces_of(meta, e, new[s], fj_buf, s, send, local)

    send_out[...] = send[:N_PART]
    local_out[...] = local[:N_EL]


def diagonal_kernel(rhs, new, local, djac, out):
    for i in range(rhs.shape[0]):
        out[i] = rhs[i] - local[i] - dot(new[i], djac[i])


def return_kernel(meta, base, recv, out, total):
    total[...] = jnp.zeros_like(total)

    @pl.loop(0, N_PART, unroll=4)
    def _(q):
        i = meta[SEND + q]
        total[i] += recv[q].astype(jnp.float32)

    for i in range(N_EL):
        out[i] = base[i] - unpack(total[i])


def shape(dims, dtype=jnp.bfloat16):
    return jax.ShapeDtypeStruct(dims, dtype)


def params(mib):
    return pltpu.CompilerParams(vmem_limit_bytes=mib * MIB)


def cost(blocks, moved):
    return pl.CostEstimate(flops=2 * blocks * R * N * N, bytes_accessed=moved, transcendentals=0)


BLOCK = 320 * 384 * 2
ROWS = (N_PART, 80, 128)
LOCAL = (N_EL, R, N)


def on_device(adjoint, adj_rhs, diag_inv, diag_jac, upper, face_jac, face_ref, send_list, colour):
    swap = [(0, 1), (1, 0)]
    core = lax.axis_index("rhs").astype(jnp.int32)
    meta = jnp.concatenate(
        [face_ref.reshape(-1), send_list.reshape(-1), colour, jnp.full((16,), core, jnp.int32)]
    )
    face_jac_other = lax.ppermute(face_jac, "rhs", swap)

    outgoing = pl.pallas_call(
        pack_kernel,
        out_shape=shape(ROWS),
        in_specs=[SMEM, VMEM],
        out_specs=VMEM,
        scratch_shapes=[pltpu.VMEM((N_EL, 80, 128), jnp.bfloat16)],
        compiler_params=params(8),
        cost_estimate=cost(0, 2 * MIB),
        name="pack_rows",
    )(meta, adjoint)
    incoming = lax.all_to_all(outgoing, "dom", split_axis=0, concat_axis=0, tiled=True)

    upper_zero = pl.pallas_call(
        select_kernel,
        out_shape=shape((C_MAX, 2, N, N)),
        in_specs=[SMEM, ANY],
        out_specs=ANY,
        scratch_shapes=[pltpu.SMEM((N_EL,), jnp.int32), pltpu.SemaphoreType.DMA((C_MAX,))],
        cost_estimate=cost(0, 32 * BLOCK),
        name="select_upper",
    )(meta, upper)
    upper_other = lax.ppermute(upper_zero, "rhs", swap)

    sent_early, local_early = pl.pallas_call(
        early_kernel,
        out_shape=(shape(ROWS), shape(LOCAL, jnp.float32)),
        in_specs=[SMEM, VMEM, ANY, ANY],
        out_specs=(VMEM, VMEM),
        scratch_shapes=[
            pltpu.SMEM((N_EL,), jnp.int32),
            pltpu.VMEM((N_PART + 1, 80, 128), jnp.bfloat16),
            pltpu.VMEM((N_EL + 1, R, N), jnp.float32),
            pltpu.VMEM((N_EL, N_FACE, N, N), jnp.bfloat16),
            pltpu.SemaphoreType.DMA((N_EL, 2)),
        ],
        compiler_params=params(28),
        cost_estimate=cost(64, 64 * BLOCK),
        name="early_faces",
    )(meta, adjoint, face_jac, face_jac_other)

    new, outbound, local = pl.pallas_call(
        sweep_kernel,
        out_shape=(shape(LOCAL), shape(ROWS), shape(LOCAL, jnp.float32)),
        in_specs=[SMEM, VMEM, VMEM, VMEM, VMEM, VMEM, ANY, ANY, ANY, ANY, ANY],
        out_specs=(VMEM, VMEM, VMEM),
        scratch_shapes=[
            pltpu.SMEM((N_EL,), jnp.int32),
            pltpu.VMEM((N_PART + 1, 80, 128), jnp.bfloat16),
            pltpu.VMEM((N_EL + 1, R, N), jnp.float32),
            pltpu.VMEM((C_MAX, R, N), jnp.bfloat16),
            pltpu.VMEM((C_MAX, R, N), jnp.bfloat16),
            pltpu.VMEM((C_MAX, N_FACE, N, N), jnp.bfloat16),
            pltpu.VMEM((C_MAX, N, N), jnp.bfloat16),
            pltpu.VMEM((C_MAX, N_FACE, N, N), jnp.bfloat16),
            pltpu.SemaphoreType.DMA((C_MAX, 2)),
            pltpu.SemaphoreType.DMA((C_MAX,)),
            pltpu.SemaphoreType.DMA((C_MAX, 2)),
        ],
        compiler_params=params(36),
        cost_estimate=cost(72, 72 * BLOCK),
        name="sweep",
    )(meta, adjoint, adj_rhs, incoming, sent_early, local_early, upper, upper_other, diag_inv,
      face_jac, face_jac_other)
    inbound = lax.all_to_all(outbound, "dom", split_axis=0, concat_axis=0, tiled=True)

    tile = pl.BlockSpec((4, R, N), lambda i: (i, 0, 0))
    base = pl.pallas_call(
        diagonal_kernel,
        out_shape=shape(LOCAL, jnp.float32),
        grid=(4,),
        in_specs=[tile, tile, tile, pl.BlockSpec((4, N, N), lambda i: (i, 0, 0))],
        out_specs=tile,
        compiler_params=params(12),
        cost_estimate=cost(16, 16 * BLOCK),
        name="diagonal",
    )(adj_rhs, new, local, diag_jac)

    residual = pl.pallas_call(
        return_kernel,
        out_shape=shape(LOCAL, jnp.float32),
        in_specs=[SMEM, VMEM, VMEM],
        out_specs=VMEM,
        scratch_shapes=[pltpu.VMEM((N_EL, 80, 128), jnp.float32)],
        compiler_params=params(8),
        cost_estimate=cost(0, 3 * MIB),
        name="return_sums",
    )(meta, base, inbound)
    return new, residual


def solution(mesh):
    in_specs = (
        P("dom", "rhs", None),
        P("dom", "rhs", None),
        P("dom", None, None),
        P("dom", None, None),
        P("dom", "rhs", None, None),
        P("dom", "rhs", None, None),
        P("dom", None),
        P("dom", None, None),
        P("dom"),
    )
    out_specs = (P("dom", "rhs", None), P("dom", "rhs", None))
    return jax.shard_map(
        on_device, mesh=mesh, in_specs=in_specs, out_specs=out_specs, check_vma=False
    )
```

time: 154 us -> 203 us (1.32)
  Pallas kernels: 0 us -> 143 us
  waiting for transfers between devices: 60.1 us -> 25.1 us
  matrix products: 23 us -> 0 us
  other arithmetic: 23.2 us -> 1.31 us
  between operations: 14.2 us -> 0.76 us
  starting transfers between devices: 21.9 us -> 16.8 us
  local copies, waits for them, and re-layouts: 11.2 us -> 14.8 us
    pallas_call x0 -> x6, Pallas kernels: none -> 143 us  [the longest x1 121 us: on_device(): pl.pallas_call(select_kernel, out_shape=shape((C_MAX, 2, N, N)), in_specs...]
    dot_general x3 -> x0, matrix products: 23 us -> none  [the longest x1 13.1 us: on_device(): jnp.einsum('ern,enm->erm', reduced, diag_inv, preferred_element_type=jnp....]
    scatter-add x2 -> x0, other arithmetic: 18.3 us -> none  [the longest x1 10.3 us: on_device(): jax.ops.segment_sum(partial_value.reshape((elem_count * face_count, width...]
    all_gather x2 -> x0, waiting for transfers between devices: 13.4 us -> none  [the longest x1 13.4 us: on_device(): segment = lax.all_gather(face_jac, 'rhs', axis=1, tiled=True)]
    unnamed x17 -> x25, local copies, waits for them, and re-layouts: 1.48 us -> 14.7 us
    all_to_all x1, waiting for transfers between devices: 23.8 us -> 10.7 us  [on_device(): lax.all_to_all(outgoing, 'dom', split_axis=0, concat_axis=0, tiled=True)]
    all_to_all x1, waiting for transfers between devices: 21.6 us -> 14.4 us  [on_device(): lax.all_to_all(outbound, 'dom', split_axis=0, concat_axis=0, tiled=True)]
    all_to_all x1, starting transfers between devices: 10.3 us -> 4.66 us  [on_device(): lax.all_to_all(outbound, 'dom', split_axis=0, concat_axis=0, tiled=True)]
  transfers between devices with their start and end apart: 4 -> 4, of which waited for: 3 -> 2; matrix products, arithmetic and copies ran while one was open for 14% -> 1% of each run, Pallas kernels for 0% -> 65%
where the time goes in v1:
time: 203 us; the launch traced here: 202 us
  Pallas kernels  143 us (70%)
  waiting for transfers between devices  25.1 us (12%)
  starting transfers between devices  16.8 us (8%)
  local copies, waits for them, and re-layouts  14.8 us (7%)
    pallas_call x1, Pallas kernels, on_device(): pl.pallas_call(select_kernel, out_shape=shape((C_MAX, 2, N, N)), in_specs...  121 us
    unnamed x25, local copies, waits for them, and re-layouts  14.7 us
    all_to_all x1, waiting for transfers between devices, on_device(): lax.all_to_all(outbound, 'dom', split_axis=0, concat_axis=0, tiled=True)  14.4 us
    all_to_all x1, starting transfers between devices, on_device(): lax.all_to_all(outgoing, 'dom', split_axis=0, concat_axis=0, tiled=True)  11.5 us
    all_to_all x1, waiting for transfers between devices, on_device(): lax.all_to_all(outgoing, 'dom', split_axis=0, concat_axis=0, tiled=True)  10.7 us
    pallas_call x1, Pallas kernels, on_device(): pl.pallas_call(sweep_kernel, out_shape=(shape(LOCAL), shape(ROWS), shape(...  10.6 us
    pallas_call x1, Pallas kernels, on_device(): pl.pallas_call(early_kernel, out_shape=(shape(ROWS), shape(LOCAL, jnp.flo...  6.64 us
    all_to_all x1, starting transfers between devices, on_device(): lax.all_to_all(outbound, 'dom', split_axis=0, concat_axis=0, tiled=True)  4.66 us
  transfers between devices with their start and end apart: 4, of which 2 were waited for; matrix products, arithmetic and copies ran while one was open for 1% of the time, Pallas kernels for 65%

profile of v1, /device:TPU:0, one launch (start us, length us, event | category | flops | bytes accessed | tf_op | source)
XLA Modules:
  0.0 202.2 jit_solution(5548780828427257654)
XLA Ops:
  0.6 0.1 collective-permute-start
  0.7 0.8 copy.12
  1.5 0.1 reshape.10
  1.6 1.3 pad_add_fusion.meta
  2.9 0.0 copy-start.3
  2.9 0.0 copy-start.11
  2.9 121.3 %select_upper.1 = bf16[8,2,320,320]{3,2,1,0:T(8,128)(2,1)} custom-call(s32[160]{0:T(256)} %pad_add_fusion.meta, bf16[16,2,320,320]{3,2,1,0:T(8,128)(2,1)} %upper.3), custom_call_target="tpu_custom_call" | custom-call | bytes 7864320 | tf_op jit(solution)/shard_map/select_upper/pallas_call | solution.py:239
  124.2 0.6 collective-permute-start.1
  124.8 0.0 copy-done.3
  124.8 0.0 copy-done.11
  124.8 1.9 pack_rows.1
  126.7 11.5 %all-to-all-start = ((bf16[64,80,128]{2,1,0:T(8,128)(2,1)}), bf16[64,80,128]{2,1,0:T(8,128)(2,1)S(1)}, u32[]{:S(2)}, u32[]{:S(2)}) async-start(bf16[64,80,128]{2,1,0:T(8,128)(2,1)} %pack_rows.1), calls=%async_computation | async-start | bytes 2621440 | tf_op jit(solution)/shard_map/all_to_all | solution.py:237
  138.2 0.0 collective-permute-done.fj_other
  138.2 0.0 copy-start
  138.2 3.2 %copy-done = bf16[16,2,320,320]{3,2,1,0:T(8,128)(2,1)S(1)} copy-done((bf16[16,2,320,320]{3,2,1,0:T(8,128)(2,1)S(1)}, bf16[16,2,320,320]{3,2,1,0:T(8,128)(2,1)}, u32[]{:S(2)}) %copy-start) | copy-done | bytes 6553624
  141.4 0.0 copy-start.4
  141.4 6.6 %early_faces.1 = (bf16[64,80,128]{2,1,0:T(8,128)(2,1)S(1)}, f32[16,32,320]{2,1,0:T(8,128)S(1)}) custom-call(s32[160]{0:T(256)S(1)} %copy-done.11, bf16[16,32,320]{2,1,0:T(8,128)(2,1)S(1)} %copy-done.3, bf16[16,2,320,320]{3,2,1,0:T(8,128)(2,1)S(1)} %copy-done, bf16[16,2,320,320]{3,2,1,0:T(8,128)(2,1)} %collective-permute-done.fj_other), custom_call_target="tpu_custom_call" | custom-call | flops 419430400 | bytes 15728640 | tf_op jit(solution)/shard_map/early_faces/pallas_call | solution.py:250
  148.1 0.0 copy-start.6
  148.1 1.0 copy-done.6
  149.1 10.7 %all-to-all-done.recv = bf16[64,80,128]{2,1,0:T(8,128)(2,1)S(1)} async-done(((bf16[64,80,128]{2,1,0:T(8,128)(2,1)}), bf16[64,80,128]{2,1,0:T(8,128)(2,1)S(1)}, u32[]{:S(2)}, u32[]{:S(2)}) %all-to-all-start) | async-done | bytes 1310752 | tf_op jit(solution)/shard_map/all_to_all | solution.py:237
  159.8 0.0 collective-permute-done.1.upper_other
  159.8 0.0 copy-done.4
  159.8 0.0 copy-start.2
  159.8 2.1 %copy-done.2 = bf16[16,320,320]{2,1,0:T(8,128)(2,1)S(1)} copy-done((bf16[16,320,320]{2,1,0:T(8,128)(2,1)S(1)}, bf16[16,320,320]{2,1,0:T(8,128)(2,1)}, u32[]{:S(2)}) %copy-start.2) | copy-done | bytes 3276824
  161.9 0.0 copy-start.7
  161.9 1.3 copy-done.7
  163.3 10.6 %sweep.1 = (bf16[16,32,320]{2,1,0:T(8,128)(2,1)}, bf16[64,80,128]{2,1,0:T(8,128)(2,1)S(1)}, f32[16,32,320]{2,1,0:T(8,128)S(1)}) custom-call(s32[160]{0:T(256)S(1)} %copy-done.11, bf16[16,32,320]{2,1,0:T(8,128)(2,1)S(1)} %copy-done.3, f32[16,32,320]{2,1,0:T(8,128)S(1)} %copy-done.4, bf16[64,80,128]{2,1,0:T(8,128)(2,1)S(1)} %all-to-all-done.recv, ...), custom_call_target="tpu_custom_call" | custom-call | flops 471859200 | bytes 17694720 | tf_op jit(solution)/shard_map/sweep/pallas_call | solution.py:267
  173.8 0.0 copy-start.5
  173.9 1.1 copy-done.5
  174.9 0.0 copy-start.8
  174.9 0.9 copy-done.8
  175.8 4.7 %all-to-all-start.1 = ((bf16[64,80,128]{2,1,0:T(8,128)(2,1)}), bf16[64,80,128]{2,1,0:T(8,128)(2,1)S(1)}, u32[]{:S(2)}, u32[]{:S(2)}) async-start(bf16[64,80,128]{2,1,0:T(8,128)(2,1)} %copy-done.5), calls=%async_computation.1 | async-start | bytes 2621440 | tf_op jit(solution)/shard_map/all_to_all | solution.py:290
  180.5 0.0 copy-start.1
  180.5 2.1 %copy-done.1 = bf16[16,320,320]{2,1,0:T(8,128)(2,1)S(1)} copy-done((bf16[16,320,320]{2,1,0:T(8,128)(2,1)S(1)}, bf16[16,320,320]{2,1,0:T(8,128)(2,1)}, u32[]{:S(2)}) %copy-start.1) | copy-done | bytes 3276824
  182.6 0.0 copy-start.9
  182.6 1.1 copy-done.9
  183.7 0.0 copy-start.10
  183.7 1.0 copy-done.10
  184.7 1.1 diagonal.1.base
  185.8 14.4 %all-to-all-done.1.recv = bf16[64,80,128]{2,1,0:T(8,128)(2,1)S(1)} async-done(((bf16[64,80,128]{2,1,0:T(8,128)(2,1)}), bf16[64,80,128]{2,1,0:T(8,128)(2,1)S(1)}, u32[]{:S(2)}, u32[]{:S(2)}) %all-to-all-start.1) | async-done | bytes 1310752 | tf_op jit(solution)/shard_map/all_to_all | solution.py:290
  200.3 2.0 return_sums.1
  (1 shorter events, 0.0 us)
Async XLA Ops:
  0.6 137.6 %collective-permute-start = (bf16[16,2,320,320]{3,2,1,0:T(8,128)(2,1)}, bf16[16,2,320,320]{3,2,1,0:T(8,128)(2,1)}, u32[]{:S(2)}, u32[]{:S(2)}) collective-permute-start(bf16[16,2,320,320]{3,2,1,0:T(8,128)(2,1)} %fj_own.3), channel_id=1, source_target_pairs={{0,1},{1,0},{2,3},{3,2},{4,5},{5,4},{6,7},{7,6},{8,9},{9,8},{10,11... | collective-permute-start | bytes 19660808 | tf_op jit(solution)/shard_map/ppermute | solution.py:225
  2.9 121.9 %copy-start.3 = (bf16[16,32,320]{2,1,0:T(8,128)(2,1)S(1)}, bf16[16,32,320]{2,1,0:T(8,128)(2,1)}, u32[]{:S(2)}) copy-start(bf16[16,32,320]{2,1,0:T(8,128)(2,1)} %adj.5) | copy-start | bytes 983044
  2.9 121.9 %copy-start.11 = (s32[160]{0:T(256)S(1)}, s32[160]{0:T(256)}, u32[]{:S(2)}) copy-start(s32[160]{0:T(256)} %pad_add_fusion.meta) | copy-start | bytes 1924
  124.2 35.6 %collective-permute-start.1 = (bf16[8,2,320,320]{3,2,1,0:T(8,128)(2,1)}, bf16[8,2,320,320]{3,2,1,0:T(8,128)(2,1)}, u32[]{:S(2)}, u32[]{:S(2)}) collective-permute-start(bf16[8,2,320,320]{3,2,1,0:T(8,128)(2,1)} %select_upper.1), channel_id=1, source_target_pairs={{0,1},{1,0},{2,3},{3,2},{4,5},{5,4},{6,7},{7,6},{8,9},{9,8},{10,11... | collective-permute-start | bytes 9830408 | tf_op jit(solution)/shard_map/ppermute | solution.py:248
  126.7 33.1 %all-to-all-start = ((bf16[64,80,128]{2,1,0:T(8,128)(2,1)}), bf16[64,80,128]{2,1,0:T(8,128)(2,1)S(1)}, u32[]{:S(2)}, u32[]{:S(2)}) async-start(bf16[64,80,128]{2,1,0:T(8,128)(2,1)} %pack_rows.1), calls=%async_computation | async-start | bytes 2621440 | tf_op jit(solution)/shard_map/all_to_all | solution.py:237
  138.2 3.2 %copy-start = (bf16[16,2,320,320]{3,2,1,0:T(8,128)(2,1)S(1)}, bf16[16,2,320,320]{3,2,1,0:T(8,128)(2,1)}, u32[]{:S(2)}) copy-start(bf16[16,2,320,320]{3,2,1,0:T(8,128)(2,1)} %fj_own.3) | copy-start | bytes 19660804
  141.4 18.4 %copy-start.4 = (f32[16,32,320]{2,1,0:T(8,128)S(1)}, f32[16,32,320]{2,1,0:T(8,128)}, u32[]{:S(2)}) copy-start(f32[16,32,320]{2,1,0:T(8,128)} %rhs.3) | copy-start | bytes 1966084
  148.1 1.1 copy-start.6
  159.8 2.1 %copy-start.2 = (bf16[16,320,320]{2,1,0:T(8,128)(2,1)S(1)}, bf16[16,320,320]{2,1,0:T(8,128)(2,1)}, u32[]{:S(2)}) copy-start(bf16[16,320,320]{2,1,0:T(8,128)(2,1)} %dinv.1) | copy-start | bytes 9830404
  161.9 1.3 copy-start.7
  173.8 1.1 copy-start.5
  174.9 0.9 copy-start.8
  175.8 24.4 %all-to-all-start.1 = ((bf16[64,80,128]{2,1,0:T(8,128)(2,1)}), bf16[64,80,128]{2,1,0:T(8,128)(2,1)S(1)}, u32[]{:S(2)}, u32[]{:S(2)}) async-start(bf16[64,80,128]{2,1,0:T(8,128)(2,1)} %copy-done.5), calls=%async_computation.1 | async-start | bytes 2621440 | tf_op jit(solution)/shard_map/all_to_all | solution.py:290
  180.5 2.1 %copy-start.1 = (bf16[16,320,320]{2,1,0:T(8,128)(2,1)S(1)}, bf16[16,320,320]{2,1,0:T(8,128)(2,1)}, u32[]{:S(2)}) copy-start(bf16[16,320,320]{2,1,0:T(8,128)(2,1)} %djac.1) | copy-start | bytes 9830404
  182.6 1.1 copy-start.9
  183.7 1.0 copy-start.10

commit v2 on v0

v2 whole, which is shorter than its diff:
```python
import jax
import jax.numpy as jnp
from jax import lax
from jax.experimental import pallas as pl
from jax.experimental.pallas import tpu as pltpu
from jax.sharding import PartitionSpec as P

N_EL, N_FACE, N_PART, C_MAX = 16, 4, 64, 8
N_JOB = C_MAX * N_FACE
R, N = 32, 320
MIB = 2**20
BF16, F32 = jnp.bfloat16, jnp.float32

SMEM = pl.BlockSpec(memory_space=pltpu.SMEM)
VMEM = pl.BlockSpec(memory_space=pltpu.VMEM)
HBM = pl.BlockSpec(memory_space=pltpu.HBM)
DMA = pltpu.SemaphoreType.DMA

ROWS = (N_PART, 80, 128)
LOCAL = (N_EL, R, N)

ELEM, JOB_S, JOB_BLOCK, JOB_AT, TABLE = 8, 32, 72, 112, 152


def dot(a, b):
    return jnp.dot(a, b, preferred_element_type=F32)


def pack(v):
    tail = jnp.concatenate([v[:16, 256:], v[16:, 256:]], axis=1)
    return jnp.concatenate([v[:, :128], v[:, 128:256], tail], axis=0)


def unpack(p):
    tail = jnp.concatenate([p[64:, :64], p[64:, 64:]], axis=0)
    return jnp.concatenate([p[:32], p[32:64], tail], axis=1)


def order_by_colour(colour, order):
    def place(e, carry):
        zeros, others = carry
        is_zero = colour[e] == 0
        order[jnp.where(is_zero, zeros, N_EL - 1 - others)] = e
        step = is_zero.astype(jnp.int32)
        return zeros + step, others + 1 - step

    return lax.fori_loop(0, N_EL, place, (jnp.int32(0), jnp.int32(0)))[0]


def pack_kernel(listed, adj, out, places, own, packed, rows, in_sem, out_sem):
    loads = [
        pltpu.make_async_copy(listed, places, in_sem.at[0]),
        pltpu.make_async_copy(adj, own, in_sem.at[1]),
    ]
    for c in loads:
        c.start()
    for c in loads:
        c.wait()
    for e in range(N_EL):
        packed[e] = pack(own[e])

    @pl.loop(0, 4)
    def _(g):
        for k in range(16):
            rows[16 * g + k] = packed[places[16 * g + k]]
        part = pl.ds(16 * g, 16)
        pltpu.make_async_copy(rows.at[part], out.at[part], out_sem).start()

    pltpu.make_async_copy(rows, out, out_sem).wait()


def landed(buf, sem):
    pltpu.make_async_copy(buf, buf, sem).wait()


def half(core_side):
    core = lax.axis_index("rhs")
    return 2 * core if core_side == 0 else 2 - 2 * core


def push_near(refs, adj, e, first, blocks):
    total = None
    for k in range(2):
        ref = refs[first + k, e]
        x = adj[jnp.minimum(ref, N_EL - 1)]
        product = dot(jnp.where(ref < N_EL, x, jnp.zeros_like(x)), blocks[k])
        total = product if total is None else total + product
    return total


def early_kernel(
    refs, colour, adj, rhs, upper, fj_own, fj_other, send_out, local_out, base_out,
    order, send, local, up_buf, buf, up_sem, sem,
):
    count = order_by_colour(colour, order)

    def up_copy(s):
        return pltpu.make_async_copy(upper.at[order[s]], up_buf.at[s], up_sem.at[s])

    @pl.loop(0, count)
    def _(s):
        up_copy(s).start()

    @pl.loop(count, N_EL)
    def _(s):
        e = order[s]
        for side, source in ((0, fj_own), (1, fj_other)):
            part = buf.at[s, pl.ds(half(side), 2)]
            pltpu.make_async_copy(source.at[e], part, sem.at[s]).start()

    send[...] = jnp.zeros_like(send)
    local[...] = jnp.zeros_like(local)

    @pl.loop(0, count)
    def _(s):
        up_copy(s).wait()
        e = order[s]
        base_out[s] = rhs[e] - push_near(refs, adj, e, half(0), up_buf[s])

    @pl.loop(count, N_EL)
    def _(s):
        landed(buf.at[s], sem.at[s])
        e = order[s]
        x = adj[e]
        for f in range(N_FACE):
            ref = refs[f, e]
            product = dot(x, buf[s, f])
            send[jnp.where(ref >= N_EL, ref - N_EL, N_PART)] = pack(product.astype(BF16))
            local[jnp.minimum(ref, N_EL)] += product

    send_out[...] = send[:N_PART]
    local_out[...] = local[:N_EL]


def near_kernel(
    refs, colour, adj, base_in, upper_other, base_out, adj_out, table, order, buf, sem
):
    count = order_by_colour(colour, order)

    def copy(s):
        return pltpu.make_async_copy(upper_other.at[order[s]], buf.at[s], sem.at[s])

    @pl.loop(0, count)
    def _(s):
        copy(s).start()

    adj_out[...] = adj[...]

    def add_jobs(first):
        def add(s, jobs):
            e = order[s]
            for k in range(2):
                ref = refs[first + k, e]

                @pl.when(ref >= N_EL)
                def _():
                    table[JOB_S + jobs] = s
                    table[JOB_BLOCK + jobs] = 2 * e + k
                    table[JOB_AT + jobs] = ref - N_EL

                jobs += (ref >= N_EL).astype(jnp.int32)
            return jobs

        return add

    own_jobs = lax.fori_loop(0, count, add_jobs(half(0)), jnp.int32(0))
    jobs = lax.fori_loop(0, count, add_jobs(half(1)), own_jobs)
    for k in range(3):
        table[JOB_S + jobs + k] = C_MAX
        table[JOB_BLOCK + jobs + k] = 0
        table[JOB_AT + jobs + k] = 0
    table[0] = count
    table[1] = own_jobs
    table[2] = jobs
    for s in range(C_MAX):
        table[ELEM + s] = order[s]

    @pl.loop(0, count)
    def _(s):
        copy(s).wait()
        base_out[s] = base_in[s] - push_near(refs, adj, order[s], half(1), buf[s])


def sweep_kernel(
    table, recv, base, upper, upper_other, dinv, fj_own, fj_other, new_in, send_in,
    new_out, send_out,
    start, total, new, row, up_buf, dinv_buf, fj_buf, up_sem, dinv_sem, fj_sem, base_sem, out_sem,
):
    del new_in, send_in
    count, own_jobs, jobs = table[0], table[1], table[2]
    groups = lax.div(jobs + 3, 4)

    def fetch(own, other, buf, sem):
        def copies(first, last, source):
            @pl.loop(first, last)
            def _(j):
                block = source.at[table[JOB_BLOCK + j]]
                pltpu.make_async_copy(block, buf.at[j], sem.at[lax.div(j, 4)]).start()

        copies(0, own_jobs, own)
        copies(own_jobs, 4 * groups, other)

    base_copy = pltpu.make_async_copy(base, start, base_sem)
    fetch(upper, upper_other, up_buf, up_sem)
    base_copy.start()
    for part in range(2):

        @pl.when(count > 4 * part)
        def _():
            for s in range(4 * part, 4 * part + 4):
                block = dinv.at[table[ELEM + s]]
                pltpu.make_async_copy(block, dinv_buf.at[s], dinv_sem.at[part]).start()

    fetch(fj_own, fj_other, fj_buf, fj_sem)
    total[...] = jnp.zeros_like(total)

    def in_groups(buf, sem, body):
        @pl.loop(0, groups)
        def _(g):
            landed(buf.at[pl.ds(4 * g, 4)], sem.at[g])
            body([4 * g + k for k in range(4)])

    def push(js):
        products = [dot(unpack(recv[table[JOB_AT + j]]), up_buf[j]) for j in js]
        for j, product in zip(js, products):
            total[table[JOB_S + j]] += product

    in_groups(up_buf, up_sem, push)
    base_copy.wait()
    for part in range(2):

        @pl.when(count > 4 * part)
        def _():
            landed(dinv_buf.at[pl.ds(4 * part, 4)], dinv_sem.at[part])
            reduced = [(start[s] - total[s]).astype(BF16) for s in range(4 * part, 4 * part + 4)]
            products = [dot(reduced[k], dinv_buf[4 * part + k]) for k in range(4)]
            for k in range(4):
                new[4 * part + k] = products[k].astype(BF16)

    def new_copy(s):
        return pltpu.make_async_copy(new.at[s], new_out.at[table[ELEM + s]], out_sem.at[0])

    def row_copy(j):
        return pltpu.make_async_copy(row.at[j], send_out.at[table[JOB_AT + j]], out_sem.at[1])

    @pl.loop(0, count)
    def _(s):
        new_copy(s).start()

    def spread(js):
        products = [dot(new[table[JOB_S + j]], fj_buf[j]) for j in js]
        for j, product in zip(js, products):
            row[j] = pack(product.astype(BF16))
        for j in js:

            @pl.when(j < jobs)
            def _():
                row_copy(j).start()

    in_groups(fj_buf, fj_sem, spread)

    @pl.loop(0, count)
    def _(s):
        new_copy(s).wait()

    @pl.loop(0, jobs)
    def _(j):
        row_copy(j).wait()


def diagonal_kernel(
    refs, colour, rhs, new, local_in, djac, fj_own, fj_other, out,
    order, local, djac_buf, fj_buf, local_sem, djac_sem, fj_sem,
):
    count = order_by_colour(colour, order)

    def djac_copy(g):
        part = pl.ds(4 * g, 4)
        return pltpu.make_async_copy(djac.at[part], djac_buf.at[part], djac_sem.at[g])

    local_copy = pltpu.make_async_copy(local_in, local.at[pl.ds(0, N_EL)], local_sem)
    local_copy.start()

    @pl.loop(0, count)
    def _(s):
        e = order[s]
        for side, source in ((0, fj_own), (1, fj_other)):
            part = fj_buf.at[s, pl.ds(half(side), 2)]
            pltpu.make_async_copy(source.at[e], part, fj_sem.at[s]).start()

    for g in range(4):
        djac_copy(g).start()
    local_copy.wait()
    local[N_EL] = jnp.zeros((R, N), F32)

    @pl.loop(0, count)
    def _(s):
        landed(fj_buf.at[s], fj_sem.at[s])
        e = order[s]
        products = [dot(new[e], fj_buf[s, f]) for f in range(N_FACE)]
        for f in range(N_FACE):
            local[jnp.minimum(refs[f, e], N_EL)] += products[f]

    @pl.loop(0, 4)
    def _(g):
        djac_copy(g).wait()
        for k in range(4):
            i = 4 * g + k
            out[i] = pack(rhs[i] - local[i] - dot(new[i], djac_buf[i]))


def return_kernel(listed, base, recv, out, places, base_buf, total, out_buf, in_sem, out_sem):
    places_copy = pltpu.make_async_copy(listed, places, in_sem.at[0])
    base_copy = pltpu.make_async_copy(base, base_buf, in_sem.at[1])
    places_copy.start()
    base_copy.start()
    total[...] = jnp.zeros_like(total)
    places_copy.wait()

    @pl.loop(0, N_PART, unroll=8)
    def _(q):
        total[places[q]] += recv[q].astype(F32)

    base_copy.wait()
    for g in range(4):
        for i in range(4 * g, 4 * g + 4):
            out_buf[i] = unpack(base_buf[i] - total[i])
        part = pl.ds(4 * g, 4)
        pltpu.make_async_copy(out_buf.at[part], out.at[part], out_sem).start()
    pltpu.make_async_copy(out_buf, out, out_sem).wait()


def call(kernel, out, in_specs, out_specs, scratch, mib, aliases=None):
    return pl.pallas_call(
        kernel,
        out_shape=out,
        in_specs=in_specs,
        out_specs=out_specs,
        scratch_shapes=scratch,
        input_output_aliases=aliases or {},
        compiler_params=pltpu.CompilerParams(vmem_limit_bytes=mib * MIB),
        cost_estimate=pl.CostEstimate(flops=0, bytes_accessed=0, transcendentals=0),
        name=kernel.__name__,
    )


def hbm(dims, dtype=BF16):
    return pltpu.HBM(dims, dtype)


def pin(a):
    return pltpu.with_memory_space_constraint(a, pltpu.HBM)


ORDER = pltpu.SMEM((N_EL,), jnp.int32)
LISTED = pltpu.SMEM((N_PART,), jnp.int32)
PACK_SCRATCH = [
    LISTED, pltpu.VMEM(LOCAL, BF16), pltpu.VMEM((N_EL, 80, 128), BF16), pltpu.VMEM(ROWS, BF16),
    DMA((2,)), DMA,
]
RETURN_SCRATCH = [
    LISTED, pltpu.VMEM((N_EL, 80, 128), F32), pltpu.VMEM((N_EL, 80, 128), F32), pltpu.VMEM(LOCAL, F32),
    DMA((2,)), DMA,
]
SWEEP_SCRATCH = [
    pltpu.VMEM((C_MAX, R, N), F32), pltpu.VMEM((C_MAX + 1, R, N), F32),
    pltpu.VMEM((C_MAX + 1, R, N), BF16), pltpu.VMEM((N_JOB, 80, 128), BF16),
    pltpu.VMEM((N_JOB, N, N), BF16), pltpu.VMEM((C_MAX, N, N), BF16), pltpu.VMEM((N_JOB, N, N), BF16),
    DMA((N_JOB // 4,)), DMA((2,)), DMA((N_JOB // 4,)), DMA, DMA((2,)),
]


def on_device(adjoint, adj_rhs, diag_inv, diag_jac, upper, face_jac, face_ref, send_list, colour):
    swap = [(0, 1), (1, 0)]
    blocks = (2 * N_EL, N, N)
    refs, listed, colour = pin(face_ref.T), pin(send_list.reshape(-1)), pin(colour)
    face_jac_other = lax.ppermute(face_jac, "rhs", swap)
    upper_other = lax.ppermute(upper, "rhs", swap)
    adj, rhs, fj, fj_other = pin(adjoint), pin(adj_rhs), pin(face_jac), pin(face_jac_other)

    outgoing = call(
        pack_kernel, hbm(ROWS), [HBM, HBM], HBM, PACK_SCRATCH,
        8,
    )(listed, adj)
    incoming = lax.all_to_all(outgoing, "dom", split_axis=0, concat_axis=0, tiled=True)

    sent, local, base_own = call(
        early_kernel, (hbm(ROWS), hbm(LOCAL, F32), hbm((C_MAX, R, N), F32)),
        [SMEM, SMEM, VMEM, VMEM, HBM, HBM, HBM], (VMEM, VMEM, VMEM),
        [ORDER, pltpu.VMEM((N_PART + 1, 80, 128), BF16), pltpu.VMEM((N_EL + 1, R, N), F32),
         pltpu.VMEM((C_MAX, 2, N, N), BF16), pltpu.VMEM((N_EL, N_FACE, N, N), BF16),
         DMA((C_MAX,)), DMA((N_EL,))],
        36,
    )(refs, colour, adj, rhs, pin(upper), fj, fj_other)

    base, kept, table = call(
        near_kernel, (hbm((C_MAX, R, N), F32), hbm(LOCAL), hbm((TABLE,), jnp.int32)),
        [SMEM, SMEM, VMEM, VMEM, HBM], (VMEM, VMEM, SMEM),
        [ORDER, pltpu.VMEM((C_MAX, 2, N, N), BF16), DMA((C_MAX,))],
        16,
    )(refs, colour, adj, pin(base_own), pin(upper_other))

    new, outbound = call(
        sweep_kernel, (hbm(LOCAL), hbm(ROWS)),
        [SMEM, VMEM, HBM, HBM, HBM, HBM, HBM, HBM, HBM, HBM], (HBM, HBM),
        SWEEP_SCRATCH,
        32, {8: 0, 9: 1},
    )(pin(table), incoming, pin(base), pin(upper.reshape(blocks)), pin(upper_other.reshape(blocks)),
      pin(diag_inv), pin(face_jac.reshape(blocks)), pin(face_jac_other.reshape(blocks)), pin(kept),
      pin(sent))
    inbound = lax.all_to_all(outbound, "dom", split_axis=0, concat_axis=0, tiled=True)

    own = call(
        diagonal_kernel, hbm((N_EL, 80, 128), F32), [SMEM, SMEM, VMEM, VMEM, HBM, HBM, HBM, HBM], VMEM,
        [ORDER, pltpu.VMEM((N_EL + 1, R, N), F32), pltpu.VMEM((N_EL, N, N), BF16),
         pltpu.VMEM((C_MAX, N_FACE, N, N), BF16), DMA, DMA((4,)), DMA((C_MAX,))],
        20,
    )(refs, colour, rhs, pin(new), pin(local), pin(diag_jac), fj, fj_other)

    residual = call(
        return_kernel, hbm(LOCAL, F32), [HBM, HBM, VMEM], HBM, RETURN_SCRATCH,
        8,
    )(listed, pin(own), inbound)
    return new, residual


def solution(mesh):
    in_specs = (
        P("dom", "rhs", None),
        P("dom", "rhs", None),
        P("dom", None, None),
        P("dom", None, None),
        P("dom", "rhs", None, None),
        P("dom", "rhs", None, None),
        P("dom", None),
        P("dom", None, None),
        P("dom"),
    )
    out_specs = (P("dom", "rhs", None), P("dom", "rhs", None))
    return jax.shard_map(
        on_device, mesh=mesh, in_specs=in_specs, out_specs=out_specs, check_vma=False
    )
```

time: 154 us -> 72.2 us (0.47)
  waiting for transfers between devices: 60.1 us -> 24.1 us
  Pallas kernels: 0 us -> 26.9 us
  other arithmetic: 23.2 us -> 0 us
  matrix products: 23 us -> 0 us
  between operations: 14.2 us -> 0.7 us
  local copies, waits for them, and re-layouts: 11.2 us -> 0 us
  starting transfers between devices: 21.9 us -> 19.5 us
    pallas_call x0 -> x6, Pallas kernels: none -> 26.9 us  [the longest x1 9.27 us: on_device(): call(early_kernel, (hbm(ROWS), hbm(LOCAL, F32), hbm((C_MAX, R, N), F32)),...]
    dot_general x3 -> x0, matrix products: 23 us -> none  [the longest x1 13.1 us: on_device(): jnp.einsum('ern,enm->erm', reduced, diag_inv, preferred_element_type=jnp....]
    scatter-add x2 -> x0, other arithmetic: 18.3 us -> none  [the longest x1 10.3 us: on_device(): jax.ops.segment_sum(partial_value.reshape((elem_count * face_count, width...]
    all_to_all x1, waiting for transfers between devices: 23.8 us -> 8.24 us  [on_device(): lax.all_to_all(outgoing, 'dom', split_axis=0, concat_axis=0, tiled=True)]
    all_gather x2 -> x0, waiting for transfers between devices: 13.4 us -> none  [the longest x1 13.4 us: on_device(): segment = lax.all_gather(face_jac, 'rhs', axis=1, tiled=True)]
    all_to_all x1, waiting for transfers between devices: 21.6 us -> 15.4 us  [on_device(): lax.all_to_all(outbound, 'dom', split_axis=0, concat_axis=0, tiled=True)]
    gather x2 -> x0, local copies, waits for them, and re-layouts: 3.85 us -> none  [the longest x1 1.93 us: on_device(): outgoing = adjoint[send_table]]
    reshape x1 -> x0, local copies, waits for them, and re-layouts: 3.27 us -> none  [on_device(): outbound = gathered[elem_count:].astype(jnp.bfloat16).reshape((part_count...]
  transfers between devices with their start and end apart: 4 -> 4, of which waited for: 3 -> 3; matrix products, arithmetic and copies ran while one was open for 14% -> 0% of each run, Pallas kernels for 0% -> 29%
where the time goes in v2:
time: 72.2 us; the launch traced here: 71.3 us
  Pallas kernels  26.9 us (37%)
  waiting for transfers between devices  24.1 us (33%)
  starting transfers between devices  19.5 us (27%)
    all_to_all x1, waiting for transfers between devices, on_device(): lax.all_to_all(outbound, 'dom', split_axis=0, concat_axis=0, tiled=True)  15.4 us
    all_to_all x1, starting transfers between devices, on_device(): lax.all_to_all(outgoing, 'dom', split_axis=0, concat_axis=0, tiled=True)  11.5 us
    pallas_call x1, Pallas kernels, on_device(): call(early_kernel, (hbm(ROWS), hbm(LOCAL, F32), hbm((C_MAX, R, N), F32)),...  9.27 us
    all_to_all x1, waiting for transfers between devices, on_device(): lax.all_to_all(outgoing, 'dom', split_axis=0, concat_axis=0, tiled=True)  8.24 us
    all_to_all x1, starting transfers between devices, on_device(): lax.all_to_all(outbound, 'dom', split_axis=0, concat_axis=0, tiled=True)  7.44 us
    pallas_call x1, Pallas kernels, on_device(): call(diagonal_kernel, hbm((N_EL, 80, 128), F32), [SMEM, SMEM, VMEM, VMEM,...  5.82 us
    pallas_call x1, Pallas kernels, on_device(): call(sweep_kernel, (hbm(LOCAL), hbm(ROWS)), [SMEM, VMEM, HBM, HBM, HBM, H...  3.86 us
    pallas_call x1, Pallas kernels, on_device(): call(near_kernel, (hbm((C_MAX, R, N), F32), hbm(LOCAL), hbm((TABLE,), jnp...  3.7 us
  transfers between devices with their start and end apart: 4, of which 3 were waited for; matrix products, arithmetic and copies ran while one was open for 0% of the time, Pallas kernels for 29%

profile of v2, /device:TPU:0, one launch (start us, length us, event | category | flops | bytes accessed | tf_op | source)
XLA Modules:
  0.0 71.3 jit_solution(9681721130592309686)
XLA Ops:
  0.6 0.1 collective-permute-start
  0.7 0.5 collective-permute-start.1
  1.2 2.2 %pack_kernel.1 = bf16[64,80,128]{2,1,0:T(8,128)(2,1)} custom-call(s32[64]{0:T(128)} %bitcast.11, bf16[16,32,320]{2,1,0:T(8,128)(2,1)} %adj.5), custom_call_target="tpu_custom_call" | custom-call | tf_op jit(solution)/shard_map/pack_kernel/pallas_call | solution.py:381
  3.4 11.5 %all-to-all-start = ((bf16[64,80,128]{2,1,0:T(8,128)(2,1)}), bf16[64,80,128]{2,1,0:T(8,128)(2,1)S(1)}, u32[]{:S(2)}, u32[]{:S(2)}) async-start(bf16[64,80,128]{2,1,0:T(8,128)(2,1)} %pack_kernel.1), calls=%async_computation | async-start | bytes 2621440 | tf_op jit(solution)/shard_map/all_to_all | solution.py:385
  15.0 0.0 collective-permute-done.fj_other
  15.0 9.3 %early_kernel.1 = (bf16[64,80,128]{2,1,0:T(8,128)(2,1)}, f32[16,32,320]{2,1,0:T(8,128)}, f32[8,32,320]{2,1,0:T(8,128)}) custom-call(s32[4,16]{1,0:T(4,128)} %bitcast.8, s32[16]{0:T(128)} %colour.5, bf16[16,32,320]{2,1,0:T(8,128)(2,1)} %adj.5, f32[16,32,320]{2,1,0:T(8,128)} %rhs.3, bf16[16,2,320,320]{3,2,1,0:T(8,128)(2,1)} %upper.1, ...), custom_call_target="tpu_custom_call" | custom-call | tf_op jit(solution)/shard_map/early_kernel/pallas_call | solution.py:387
  24.2 0.5 collective-permute-done.1.upper_other
  24.7 3.7 %near_kernel.1 = (f32[8,32,320]{2,1,0:T(8,128)}, bf16[16,32,320]{2,1,0:T(8,128)(2,1)}, s32[152]{0:T(256)}) custom-call(s32[4,16]{1,0:T(4,128)} %bitcast.9, s32[16]{0:T(128)} %colour.5, bf16[16,32,320]{2,1,0:T(8,128)(2,1)} %adj.5, f32[8,32,320]{2,1,0:T(8,128)} %get-tuple-element.10.base_in, bf16[16,2,320,320]{3,2,1,0:T(8,128)(2,1)} %collective-permute-done.1.upper_other), custom_call_target="tpu_custom_call" | custom-call | tf_op jit(solution)/shard_map/near_kernel/pallas_call | solution.py:396
  28.4 8.2 %all-to-all-done.recv = bf16[64,80,128]{2,1,0:T(8,128)(2,1)S(1)} async-done(((bf16[64,80,128]{2,1,0:T(8,128)(2,1)}), bf16[64,80,128]{2,1,0:T(8,128)(2,1)S(1)}, u32[]{:S(2)}, u32[]{:S(2)}) %all-to-all-start) | async-done | bytes 1310752 | tf_op jit(solution)/shard_map/all_to_all | solution.py:385
  36.7 3.9 %sweep_kernel.1 = (bf16[16,32,320]{2,1,0:T(8,128)(2,1)}, bf16[64,80,128]{2,1,0:T(8,128)(2,1)}) custom-call(s32[152]{0:T(256)} %get-tuple-element.11.table, bf16[64,80,128]{2,1,0:T(8,128)(2,1)S(1)} %all-to-all-done.recv, f32[8,32,320]{2,1,0:T(8,128)} %get-tuple-element.12.base, ...), custom_call_target="tpu_custom_call", output_to_operand_aliasing={{0}: (8, {}), {1}: (9, {})} | custom-call | tf_op jit(solution)/shard_map/sweep_kernel/pallas_call | solution.py:403
  40.5 7.4 %all-to-all-start.1 = ((bf16[64,80,128]{2,1,0:T(8,128)(2,1)}), bf16[64,80,128]{2,1,0:T(8,128)(2,1)S(1)}, u32[]{:S(2)}, u32[]{:S(2)}) async-start(bf16[64,80,128]{2,1,0:T(8,128)(2,1)} %get-tuple-element.17), calls=%async_computation.1 | async-start | bytes 2621440 | tf_op jit(solution)/shard_map/all_to_all | solution.py:411
  48.0 5.8 %diagonal_kernel.1.base = f32[16,80,128]{2,1,0:T(8,128)} custom-call(s32[4,16]{1,0:T(4,128)} %bitcast.10, s32[16]{0:T(128)} %colour.5, f32[16,32,320]{2,1,0:T(8,128)} %rhs.3, bf16[16,32,320]{2,1,0:T(8,128)(2,1)} %get-tuple-element.8.new, f32[16,32,320]{2,1,0:T(8,128)} %get-tuple-element.16.local_in, bf16[16,320,320]{2,1,0:T(8,128)(2,1)} %djac.1, ...), custom_call_target="tpu_custom_call" | custom-call | tf_op jit(solution)/shard_map/diagonal_kernel/pallas_call | solution.py:413
  53.8 15.4 %all-to-all-done.1.recv = bf16[64,80,128]{2,1,0:T(8,128)(2,1)S(1)} async-done(((bf16[64,80,128]{2,1,0:T(8,128)(2,1)}), bf16[64,80,128]{2,1,0:T(8,128)(2,1)S(1)}, u32[]{:S(2)}, u32[]{:S(2)}) %all-to-all-start.1) | async-done | bytes 1310752 | tf_op jit(solution)/shard_map/all_to_all | solution.py:411
  69.2 2.1 %return_kernel.1 = f32[16,32,320]{2,1,0:T(8,128)} custom-call(s32[64]{0:T(128)} %bitcast.12, f32[16,80,128]{2,1,0:T(8,128)} %diagonal_kernel.1.base, bf16[64,80,128]{2,1,0:T(8,128)(2,1)S(1)} %all-to-all-done.1.recv), custom_call_target="tpu_custom_call" | custom-call | tf_op jit(solution)/shard_map/return_kernel/pallas_call | solution.py:420
Async XLA Ops:
  0.6 14.3 %collective-permute-start = (bf16[16,2,320,320]{3,2,1,0:T(8,128)(2,1)}, bf16[16,2,320,320]{3,2,1,0:T(8,128)(2,1)}, u32[]{:S(2)}, u32[]{:S(2)}) collective-permute-start(bf16[16,2,320,320]{3,2,1,0:T(8,128)(2,1)} %fj_own.3), channel_id=1, source_target_pairs={{0,1},{1,0},{2,3},{3,2},{4,5},{5,4},{6,7},{7,6},{8,9},{9,8},{10,11... | collective-permute-start | bytes 19660808 | tf_op jit(solution)/shard_map/ppermute | solution.py:377
  0.7 24.0 %collective-permute-start.1 = (bf16[16,2,320,320]{3,2,1,0:T(8,128)(2,1)}, bf16[16,2,320,320]{3,2,1,0:T(8,128)(2,1)}, u32[]{:S(2)}, u32[]{:S(2)}) collective-permute-start(bf16[16,2,320,320]{3,2,1,0:T(8,128)(2,1)} %upper.1), channel_id=1, source_target_pairs={{0,1},{1,0},{2,3},{3,2},{4,5},{5,4},{6,7},{7,6},{8,9},{9,8},{10,11... | collective-permute-start | bytes 19660808 | tf_op jit(solution)/shard_map/ppermute | solution.py:378
  3.4 33.2 %all-to-all-start = ((bf16[64,80,128]{2,1,0:T(8,128)(2,1)}), bf16[64,80,128]{2,1,0:T(8,128)(2,1)S(1)}, u32[]{:S(2)}, u32[]{:S(2)}) async-start(bf16[64,80,128]{2,1,0:T(8,128)(2,1)} %pack_kernel.1), calls=%async_computation | async-start | bytes 2621440 | tf_op jit(solution)/shard_map/all_to_all | solution.py:385
  40.5 28.7 %all-to-all-start.1 = ((bf16[64,80,128]{2,1,0:T(8,128)(2,1)}), bf16[64,80,128]{2,1,0:T(8,128)(2,1)S(1)}, u32[]{:S(2)}, u32[]{:S(2)}) async-start(bf16[64,80,128]{2,1,0:T(8,128)(2,1)} %get-tuple-element.17), calls=%async_computation.1 | async-start | bytes 2621440 | tf_op jit(solution)/shard_map/all_to_all | solution.py:411

commit v3 on v2

--- a/solution.py
+++ b/solution.py
@@ -19,7 +19,8 @@
 ROWS = (N_PART, 80, 128)
 LOCAL = (N_EL, R, N)
 
-ELEM, JOB_S, JOB_BLOCK, JOB_AT, TABLE = 8, 32, 72, 112, 152
+ELEM, JOB_S, JOB_BLOCK, JOB_AT = 8, 32, 72, 112
+NEAR_S, NEAR_BLOCK, NEAR_AT, LIST, TABLE = 152, 176, 200, 224, 288
 
 
 def dot(a, b):
@@ -78,18 +79,9 @@
     return 2 * core if core_side == 0 else 2 - 2 * core
 
 
-def push_near(refs, adj, e, first, blocks):
-    total = None
-    for k in range(2):
-        ref = refs[first + k, e]
-        x = adj[jnp.minimum(ref, N_EL - 1)]
-        product = dot(jnp.where(ref < N_EL, x, jnp.zeros_like(x)), blocks[k])
-        total = product if total is None else total + product
-    return total
-
-
 def early_kernel(
-    refs, colour, adj, rhs, upper, fj_own, fj_other, send_out, local_out, base_out,
+    refs, colour, listed, adj, rhs, upper, fj_own, fj_other,
+    send_out, local_out, base_out, adj_out, table,
     order, send, local, up_buf, buf, up_sem, sem,
 ):
     count = order_by_colour(colour, order)
@@ -110,12 +102,57 @@
 
     send[...] = jnp.zeros_like(send)
     local[...] = jnp.zeros_like(local)
+    adj_out[...] = adj[...]
+
+    def list_faces(side, remote, places, start):
+        def add(s, jobs):
+            e = order[s]
+            for k in range(2):
+                ref = refs[half(side) + k, e]
+                wanted = ref >= N_EL if remote else ref < N_EL
+
+                @pl.when(wanted)
+                def _():
+                    table[places[0] + jobs] = s
+                    table[places[1] + jobs] = 2 * e + k
+                    table[places[2] + jobs] = ref - N_EL if remote else ref
+
+                jobs += wanted.astype(jnp.int32)
+            return jobs
+
+        return lax.fori_loop(0, count, add, start)
+
+    def close(places, jobs):
+        for k in range(3):
+            table[places[0] + jobs + k] = C_MAX
+            table[places[1] + jobs + k] = 0
+            table[places[2] + jobs + k] = 0
+
+    far, near = (JOB_S, JOB_BLOCK, JOB_AT), (NEAR_S, NEAR_BLOCK, NEAR_AT)
+    own_jobs = list_faces(0, True, far, jnp.int32(0))
+    jobs = list_faces(1, True, far, own_jobs)
+    near_jobs = list_faces(1, False, near, jnp.int32(0))
+    close(far, jobs)
+    close(near, near_jobs)
+    for k, number in enumerate((count, own_jobs, jobs, near_jobs)):
+        table[k] = number
+    for s in range(C_MAX):
+        table[ELEM + s] = order[s]
+
+    @pl.loop(0, N_PART)
+    def _(q):
+        table[LIST + q] = listed[q]
 
     @pl.loop(0, count)
     def _(s):
         up_copy(s).wait()
         e = order[s]
-        base_out[s] = rhs[e] - push_near(refs, adj, e, half(0), up_buf[s])
+        total = rhs[e]
+        for k in range(2):
+            ref = refs[half(0) + k, e]
+            x = adj[jnp.minimum(ref, N_EL - 1)]
+            total -= dot(jnp.where(ref < N_EL, x, jnp.zeros_like(x)), up_buf[s, k])
+        base_out[s] = total
 
     @pl.loop(count, N_EL)
     def _(s):
@@ -132,61 +169,53 @@
     local_out[...] = local[:N_EL]
 
 
-def near_kernel(
-    refs, colour, adj, base_in, upper_other, base_out, adj_out, table, order, buf, sem
-):
-    count = order_by_colour(colour, order)
-
-    def copy(s):
-        return pltpu.make_async_copy(upper_other.at[order[s]], buf.at[s], sem.at[s])
-
-    @pl.loop(0, count)
-    def _(s):
-        copy(s).start()
-
-    adj_out[...] = adj[...]
-
-    def add_jobs(first):
-        def add(s, jobs):
-            e = order[s]
-            for k in range(2):
-                ref = refs[first + k, e]
-
-                @pl.when(ref >= N_EL)
-                def _():
-                    table[JOB_S + jobs] = s
-                    table[JOB_BLOCK + jobs] = 2 * e + k
-                    table[JOB_AT + jobs] = ref - N_EL
-
-                jobs += (ref >= N_EL).astype(jnp.int32)
-            return jobs
-
-        return add
-
-    own_jobs = lax.fori_loop(0, count, add_jobs(half(0)), jnp.int32(0))
-    jobs = lax.fori_loop(0, count, add_jobs(half(1)), own_jobs)
-    for k in range(3):
-        table[JOB_S + jobs + k] = C_MAX
-        table[JOB_BLOCK + jobs + k] = 0
-        table[JOB_AT + jobs + k] = 0
-    table[0] = count
-    table[1] = own_jobs
-    table[2] = jobs
-    for s in range(C_MAX):
-        table[ELEM + s] = order[s]
-
-    @pl.loop(0, count)
-    def _(s):
-        copy(s).wait()
-        base_out[s] = base_in[s] - push_near(refs, adj, order[s], half(1), buf[s])
+def arrive(jobs, buf, sem, g):
+    left = jobs - 4 * g
+    for n in range(1, 5):
+
+        @pl.when(left == n if n < 4 else left >= n)
+        def _():
+            landed(buf.at[pl.ds(4 * g, n)], sem.at[g])
+
+
+def near_kernel(table, adj, base, upper_other, out, own, total, buf, in_sem, sem, out_sem):
+    jobs = table[3]
+    adj_copy = pltpu.make_async_copy(adj, own, in_sem.at[0])
+    base_copy = pltpu.make_async_copy(base, total.at[pl.ds(0, C_MAX)], in_sem.at[1])
+
+    @pl.loop(0, jobs)
+    def _(j):
+        block = upper_other.at[table[NEAR_BLOCK + j]]
+        pltpu.make_async_copy(block, buf.at[j], sem.at[lax.div(j, 4)]).start()
+
+    adj_copy.start()
+    base_copy.start()
+    adj_copy.wait()
+    base_copy.wait()
+
+    @pl.loop(0, lax.div(jobs + 3, 4))
+    def _(g):
+        arrive(jobs, buf, sem, g)
+        js = [4 * g + k for k in range(4)]
+        products = [dot(own[table[NEAR_AT + j]], buf[j]) for j in js]
+        for j, product in zip(js, products):
+            total[table[NEAR_S + j]] -= product
+
+    out_copy = pltpu.make_async_copy(total.at[pl.ds(0, C_MAX)], out, out_sem)
+    out_copy.start()
+    out_copy.wait()
 
 
 def sweep_kernel(
-    table, recv, base, upper, upper_other, dinv, fj_own, fj_other, new_in, send_in,
+    table_in, recv, base, upper, upper_other, dinv, fj_own, fj_other, new_in, send_in,
     new_out, send_out,
-    start, total, new, row, up_buf, dinv_buf, fj_buf, up_sem, dinv_sem, fj_sem, base_sem, out_sem,
+    table, start, total, new, row, up_buf, dinv_buf, fj_buf, up_sem, dinv_sem, fj_sem, base_sem, out_sem,
 ):
     del new_in, send_in
+    table_copy = pltpu.make_async_copy(table_in, table, out_sem.at[0])
+    table_copy.start()
+    total[...] = jnp.zeros_like(total)
+    table_copy.wait()
     count, own_jobs, jobs = table[0], table[1], table[2]
     groups = lax.div(jobs + 3, 4)
 
@@ -198,7 +227,7 @@
                 pltpu.make_async_copy(block, buf.at[j], sem.at[lax.div(j, 4)]).start()
 
         copies(0, own_jobs, own)
-        copies(own_jobs, 4 * groups, other)
+        copies(own_jobs, jobs, other)
 
     base_copy = pltpu.make_async_copy(base, start, base_sem)
     fetch(upper, upper_other, up_buf, up_sem)
@@ -212,12 +241,11 @@
                 pltpu.make_async_copy(block, dinv_buf.at[s], dinv_sem.at[part]).start()
 
     fetch(fj_own, fj_other, fj_buf, fj_sem)
-    total[...] = jnp.zeros_like(total)
 
     def in_groups(buf, sem, body):
         @pl.loop(0, groups)
         def _(g):
-            landed(buf.at[pl.ds(4 * g, 4)], sem.at[g])
+            arrive(jobs, buf, sem, g)
             body([4 * g + k for k in range(4)])
 
     def push(js):
@@ -227,15 +255,22 @@
 
     in_groups(up_buf, up_sem, push)
     base_copy.wait()
-    for part in range(2):
-
-        @pl.when(count > 4 * part)
-        def _():
-            landed(dinv_buf.at[pl.ds(4 * part, 4)], dinv_sem.at[part])
-            reduced = [(start[s] - total[s]).astype(BF16) for s in range(4 * part, 4 * part + 4)]
-            products = [dot(reduced[k], dinv_buf[4 * part + k]) for k in range(4)]
-            for k in range(4):
-                new[4 * part + k] = products[k].astype(BF16)
+    def solve(slots):
+        reduced = [(start[s] - total[s]).astype(BF16) for s in slots]
+        products = [dot(r, dinv_buf[s]) for r, s in zip(reduced, slots)]
+        for s, product in zip(slots, products):
+            new[s] = product.astype(BF16)
+
+    landed(dinv_buf.at[pl.ds(0, 4)], dinv_sem.at[0])
+
+    @pl.when(count <= 4)
+    def _():
+        solve(range(4))
+
+    @pl.when(count > 4)
+    def _():
+        landed(dinv_buf.at[pl.ds(4, 4)], dinv_sem.at[1])
+        solve(range(8))
 
     def new_copy(s):
         return pltpu.make_async_copy(new.at[s], new_out.at[table[ELEM + s]], out_sem.at[0])
@@ -257,7 +292,16 @@
             def _():
                 row_copy(j).start()
 
-    in_groups(fj_buf, fj_sem, spread)
+    @pl.loop(0, lax.div(groups, 2))
+    def _(h):
+        for g in (2 * h, 2 * h + 1):
+            arrive(jobs, fj_buf, fj_sem, g)
+        spread([8 * h + k for k in range(8)])
+
+    @pl.when(lax.rem(groups, 2) == 1)
+    def _():
+        arrive(jobs, fj_buf, fj_sem, groups - 1)
+        spread([4 * (groups - 1) + k for k in range(4)])
 
     @pl.loop(0, count)
     def _(s):
@@ -309,17 +353,17 @@
             out[i] = pack(rhs[i] - local[i] - dot(new[i], djac_buf[i]))
 
 
-def return_kernel(listed, base, recv, out, places, base_buf, total, out_buf, in_sem, out_sem):
-    places_copy = pltpu.make_async_copy(listed, places, in_sem.at[0])
+def return_kernel(table_in, base, recv, out, table, base_buf, total, out_buf, in_sem, out_sem):
+    table_copy = pltpu.make_async_copy(table_in, table, in_sem.at[0])
     base_copy = pltpu.make_async_copy(base, base_buf, in_sem.at[1])
-    places_copy.start()
+    table_copy.start()
     base_copy.start()
     total[...] = jnp.zeros_like(total)
-    places_copy.wait()
+    table_copy.wait()
 
     @pl.loop(0, N_PART, unroll=8)
     def _(q):
-        total[places[q]] += recv[q].astype(F32)
+        total[table[LIST + q]] += recv[q].astype(F32)
 
     base_copy.wait()
     for g in range(4):
@@ -359,10 +403,11 @@
     DMA((2,)), DMA,
 ]
 RETURN_SCRATCH = [
-    LISTED, pltpu.VMEM((N_EL, 80, 128), F32), pltpu.VMEM((N_EL, 80, 128), F32), pltpu.VMEM(LOCAL, F32),
-    DMA((2,)), DMA,
+    pltpu.SMEM((TABLE,), jnp.int32),
+    pltpu.VMEM((N_EL, 80, 128), F32), pltpu.VMEM((N_EL, 80, 128), F32), pltpu.VMEM(LOCAL, F32), DMA((2,)), DMA,
 ]
 SWEEP_SCRATCH = [
+    pltpu.SMEM((TABLE,), jnp.int32),
     pltpu.VMEM((C_MAX, R, N), F32), pltpu.VMEM((C_MAX + 1, R, N), F32),
     pltpu.VMEM((C_MAX + 1, R, N), BF16), pltpu.VMEM((N_JOB, 80, 128), BF16),
     pltpu.VMEM((N_JOB, N, N), BF16), pltpu.VMEM((C_MAX, N, N), BF16), pltpu.VMEM((N_JOB, N, N), BF16),
@@ -384,28 +429,30 @@
     )(listed, adj)
     incoming = lax.all_to_all(outgoing, "dom", split_axis=0, concat_axis=0, tiled=True)
 
-    sent, local, base_own = call(
-        early_kernel, (hbm(ROWS), hbm(LOCAL, F32), hbm((C_MAX, R, N), F32)),
-        [SMEM, SMEM, VMEM, VMEM, HBM, HBM, HBM], (VMEM, VMEM, VMEM),
+    sent, local, base_own, kept, table = call(
+        early_kernel,
+        (hbm(ROWS), hbm(LOCAL, F32), hbm((C_MAX, R, N), F32), hbm(LOCAL),
+         jax.ShapeDtypeStruct((TABLE,), jnp.int32)),
+        [SMEM, SMEM, SMEM, VMEM, VMEM, HBM, HBM, HBM], (VMEM, VMEM, VMEM, VMEM, SMEM),
         [ORDER, pltpu.VMEM((N_PART + 1, 80, 128), BF16), pltpu.VMEM((N_EL + 1, R, N), F32),
          pltpu.VMEM((C_MAX, 2, N, N), BF16), pltpu.VMEM((N_EL, N_FACE, N, N), BF16),
          DMA((C_MAX,)), DMA((N_EL,))],
         36,
-    )(refs, colour, adj, rhs, pin(upper), fj, fj_other)
-
-    base, kept, table = call(
-        near_kernel, (hbm((C_MAX, R, N), F32), hbm(LOCAL), hbm((TABLE,), jnp.int32)),
-        [SMEM, SMEM, VMEM, VMEM, HBM], (VMEM, VMEM, SMEM),
-        [ORDER, pltpu.VMEM((C_MAX, 2, N, N), BF16), DMA((C_MAX,))],
-        16,
-    )(refs, colour, adj, pin(base_own), pin(upper_other))
+    )(refs, colour, listed, adj, rhs, pin(upper), fj, fj_other)
+
+    base = call(
+        near_kernel, hbm((C_MAX, R, N), F32), [SMEM, HBM, HBM, HBM], HBM,
+        [pltpu.VMEM(LOCAL, BF16), pltpu.VMEM((C_MAX + 1, R, N), F32),
+         pltpu.VMEM((2 * C_MAX, N, N), BF16), DMA((2,)), DMA((C_MAX // 2,)), DMA],
+        8,
+    )(table, adj, pin(base_own), pin(upper_other.reshape(blocks)))
 
     new, outbound = call(
         sweep_kernel, (hbm(LOCAL), hbm(ROWS)),
-        [SMEM, VMEM, HBM, HBM, HBM, HBM, HBM, HBM, HBM, HBM], (HBM, HBM),
+        [VMEM, VMEM, HBM, HBM, HBM, HBM, HBM, HBM, HBM, HBM], (HBM, HBM),
         SWEEP_SCRATCH,
         32, {8: 0, 9: 1},
-    )(pin(table), incoming, pin(base), pin(upper.reshape(blocks)), pin(upper_other.reshape(blocks)),
+    )(table, incoming, pin(base), pin(upper.reshape(blocks)), pin(upper_other.reshape(blocks)),
       pin(diag_inv), pin(face_jac.reshape(blocks)), pin(face_jac_other.reshape(blocks)), pin(kept),
       pin(sent))
     inbound = lax.all_to_all(outbound, "dom", split_axis=0, concat_axis=0, tiled=True)
@@ -418,9 +465,9 @@
     )(refs, colour, rhs, pin(new), pin(local), pin(diag_jac), fj, fj_other)
 
     residual = call(
-        return_kernel, hbm(LOCAL, F32), [HBM, HBM, VMEM], HBM, RETURN_SCRATCH,
+        return_kernel, hbm(LOCAL, F32), [VMEM, HBM, VMEM], HBM, RETURN_SCRATCH,
         8,
-    )(listed, pin(own), inbound)
+    )(table, pin(own), inbound)
     return new, residual
 
 

time: 72.2 us -> 70.4 us (0.975)
  starting transfers between devices: 19.5 us -> 17.7 us
    all_to_all x1, starting transfers between devices: 7.44 us -> 5.61 us  [on_device(): lax.all_to_all(outbound, 'dom', split_axis=0, concat_axis=0, tiled=True)]
    all_to_all x1, waiting for transfers between devices: 8.24 us -> 9.44 us  [on_device(): lax.all_to_all(outgoing, 'dom', split_axis=0, concat_axis=0, tiled=True)]
    all_to_all x1, waiting for transfers between devices: 15.4 us -> 14.3 us  [on_device(): lax.all_to_all(outbound, 'dom', split_axis=0, concat_axis=0, tiled=True)]
where the time goes in v3:
time: 70.4 us; the launch traced here: 69.9 us
  Pallas kernels  27.1 us (38%)
  waiting for transfers between devices  24.4 us (35%)
  starting transfers between devices  17.7 us (25%)
    all_to_all x1, waiting for transfers between devices, on_device(): lax.all_to_all(outbound, 'dom', split_axis=0, concat_axis=0, tiled=True)  14.3 us
    all_to_all x1, starting transfers between devices, on_device(): lax.all_to_all(outgoing, 'dom', split_axis=0, concat_axis=0, tiled=True)  11.5 us
    all_to_all x1, waiting for transfers between devices, on_device(): lax.all_to_all(outgoing, 'dom', split_axis=0, concat_axis=0, tiled=True)  9.44 us
    pallas_call x1, Pallas kernels, on_device(): call(early_kernel, (hbm(ROWS), hbm(LOCAL, F32), hbm((C_MAX, R, N), F32),...  9.1 us
    pallas_call x1, Pallas kernels, on_device(): call(diagonal_kernel, hbm((N_EL, 80, 128), F32), [SMEM, SMEM, VMEM, VMEM,...  6.39 us
    all_to_all x1, starting transfers between devices, on_device(): lax.all_to_all(outbound, 'dom', split_axis=0, concat_axis=0, tiled=True)  5.61 us
    pallas_call x1, Pallas kernels, on_device(): call(sweep_kernel, (hbm(LOCAL), hbm(ROWS)), [VMEM, VMEM, HBM, HBM, HBM, H...  4.87 us
    pallas_call x1, Pallas kernels, on_device(): call(near_kernel, hbm((C_MAX, R, N), F32), [SMEM, HBM, HBM, HBM], HBM, [p...  2.49 us
  transfers between devices with their start and end apart: 4, of which 3 were waited for; matrix products, arithmetic and copies ran while one was open for 0% of the time, Pallas kernels for 29%

profile of v3, /device:TPU:0, one launch (start us, length us, event | category | flops | bytes accessed | tf_op | source)
XLA Modules:
  0.0 69.9 jit_solution(4565186108088719134)
XLA Ops:
  0.6 0.1 collective-permute-start
  0.7 0.5 collective-permute-start.1
  1.2 2.2 %pack_kernel.1 = bf16[64,80,128]{2,1,0:T(8,128)(2,1)} custom-call(s32[64]{0:T(128)} %bitcast.10, bf16[16,32,320]{2,1,0:T(8,128)(2,1)} %adj.5), custom_call_target="tpu_custom_call" | custom-call | tf_op jit(solution)/shard_map/pack_kernel/pallas_call | solution.py:426
  3.4 11.5 %all-to-all-start = ((bf16[64,80,128]{2,1,0:T(8,128)(2,1)}), bf16[64,80,128]{2,1,0:T(8,128)(2,1)S(1)}, u32[]{:S(2)}, u32[]{:S(2)}) async-start(bf16[64,80,128]{2,1,0:T(8,128)(2,1)} %pack_kernel.1), calls=%async_computation | async-start | bytes 2621440 | tf_op jit(solution)/shard_map/all_to_all | solution.py:430
  15.0 0.0 collective-permute-done.fj_other
  15.0 9.1 %early_kernel.1 = (bf16[64,80,128]{2,1,0:T(8,128)(2,1)}, f32[16,32,320]{2,1,0:T(8,128)}, f32[8,32,320]{2,1,0:T(8,128)}, bf16[16,32,320]{2,1,0:T(8,128)(2,1)}, s32[288]{0:T(512)S(1)}) custom-call(s32[4,16]{1,0:T(4,128)} %bitcast.8, s32[16]{0:T(128)} %colour.3, s32[64]{0:T(128)} %bitcast.11, bf16[16,32,320]{2,1,0:T(8,128)(2,1)} %adj.5, f32[16,32,320]{2,1,0:T(8,128)} %rhs.3, ...), custom_call_target="tpu_custom_call" | custom-call | tf_op jit(solution)/shard_map/early_kernel/pallas_call | solution.py:432
  24.1 0.6 collective-permute-done.1
  24.7 2.5 %near_kernel.1.base = f32[8,32,320]{2,1,0:T(8,128)} custom-call(s32[288]{0:T(512)S(1)} %get-tuple-element.9.table.table_in, bf16[16,32,320]{2,1,0:T(8,128)(2,1)} %adj.5, f32[8,32,320]{2,1,0:T(8,128)} %get-tuple-element.10.base, bf16[32,320,320]{2,1,0:T(8,128)(2,1)} %bitcast.2.upper_other), custom_call_target="tpu_custom_call" | custom-call | tf_op jit(solution)/shard_map/near_kernel/pallas_call | solution.py:443
  27.2 9.4 %all-to-all-done.recv = bf16[64,80,128]{2,1,0:T(8,128)(2,1)S(1)} async-done(((bf16[64,80,128]{2,1,0:T(8,128)(2,1)}), bf16[64,80,128]{2,1,0:T(8,128)(2,1)S(1)}, u32[]{:S(2)}, u32[]{:S(2)}) %all-to-all-start) | async-done | bytes 1310752 | tf_op jit(solution)/shard_map/all_to_all | solution.py:430
  36.7 4.9 %sweep_kernel.1 = (bf16[16,32,320]{2,1,0:T(8,128)(2,1)}, bf16[64,80,128]{2,1,0:T(8,128)(2,1)}) custom-call(s32[288]{0:T(512)S(1)} %get-tuple-element.9.table.table_in, bf16[64,80,128]{2,1,0:T(8,128)(2,1)S(1)} %all-to-all-done.recv, f32[8,32,320]{2,1,0:T(8,128)} %near_kernel.1.base, ...), custom_call_target="tpu_custom_call", output_to_operand_aliasing={{0}: (8, {}), {1}: (9, {})} | custom-call | tf_op jit(solution)/shard_map/sweep_kernel/pallas_call | solution.py:450
  41.5 5.6 %all-to-all-start.1 = ((bf16[64,80,128]{2,1,0:T(8,128)(2,1)}), bf16[64,80,128]{2,1,0:T(8,128)(2,1)S(1)}, u32[]{:S(2)}, u32[]{:S(2)}) async-start(bf16[64,80,128]{2,1,0:T(8,128)(2,1)} %get-tuple-element.15), calls=%async_computation.1 | async-start | bytes 2621440 | tf_op jit(solution)/shard_map/all_to_all | solution.py:458
  47.1 6.4 %diagonal_kernel.1.base = f32[16,80,128]{2,1,0:T(8,128)} custom-call(s32[4,16]{1,0:T(4,128)} %bitcast.9, s32[16]{0:T(128)} %colour.3, f32[16,32,320]{2,1,0:T(8,128)} %rhs.3, bf16[16,32,320]{2,1,0:T(8,128)(2,1)} %get-tuple-element.7.new, f32[16,32,320]{2,1,0:T(8,128)} %get-tuple-element.14.local_in, bf16[16,320,320]{2,1,0:T(8,128)(2,1)} %djac.1, ...), custom_call_target="tpu_custom_call" | custom-call | tf_op jit(solution)/shard_map/diagonal_kernel/pallas_call | solution.py:460
  53.5 14.3 %all-to-all-done.1.recv = bf16[64,80,128]{2,1,0:T(8,128)(2,1)S(1)} async-done(((bf16[64,80,128]{2,1,0:T(8,128)(2,1)}), bf16[64,80,128]{2,1,0:T(8,128)(2,1)S(1)}, u32[]{:S(2)}, u32[]{:S(2)}) %all-to-all-start.1) | async-done | bytes 1310752 | tf_op jit(solution)/shard_map/all_to_all | solution.py:458
  67.8 2.1 %return_kernel.1 = f32[16,32,320]{2,1,0:T(8,128)} custom-call(s32[288]{0:T(512)S(1)} %get-tuple-element.9.table.table_in, f32[16,80,128]{2,1,0:T(8,128)} %diagonal_kernel.1.base, bf16[64,80,128]{2,1,0:T(8,128)(2,1)S(1)} %all-to-all-done.1.recv), custom_call_target="tpu_custom_call" | custom-call | tf_op jit(solution)/shard_map/return_kernel/pallas_call | solution.py:467
Async XLA Ops:
  0.6 14.3 %collective-permute-start = (bf16[16,2,320,320]{3,2,1,0:T(8,128)(2,1)}, bf16[16,2,320,320]{3,2,1,0:T(8,128)(2,1)}, u32[]{:S(2)}, u32[]{:S(2)}) collective-permute-start(bf16[16,2,320,320]{3,2,1,0:T(8,128)(2,1)} %fj_own.3), channel_id=1, source_target_pairs={{0,1},{1,0},{2,3},{3,2},{4,5},{5,4},{6,7},{7,6},{8,9},{9,8},{10,11... | collective-permute-start | bytes 19660808 | tf_op jit(solution)/shard_map/ppermute | solution.py:422
  0.7 24.0 %collective-permute-start.1 = (bf16[16,2,320,320]{3,2,1,0:T(8,128)(2,1)}, bf16[16,2,320,320]{3,2,1,0:T(8,128)(2,1)}, u32[]{:S(2)}, u32[]{:S(2)}) collective-permute-start(bf16[16,2,320,320]{3,2,1,0:T(8,128)(2,1)} %upper.1), channel_id=1, source_target_pairs={{0,1},{1,0},{2,3},{3,2},{4,5},{5,4},{6,7},{7,6},{8,9},{9,8},{10,11... | collective-permute-start | bytes 19660808 | tf_op jit(solution)/shard_map/ppermute | solution.py:423
  3.4 33.2 %all-to-all-start = ((bf16[64,80,128]{2,1,0:T(8,128)(2,1)}), bf16[64,80,128]{2,1,0:T(8,128)(2,1)S(1)}, u32[]{:S(2)}, u32[]{:S(2)}) async-start(bf16[64,80,128]{2,1,0:T(8,128)(2,1)} %pack_kernel.1), calls=%async_computation | async-start | bytes 2621440 | tf_op jit(solution)/shard_map/all_to_all | solution.py:430
  41.5 26.3 %all-to-all-start.1 = ((bf16[64,80,128]{2,1,0:T(8,128)(2,1)}), bf16[64,80,128]{2,1,0:T(8,128)(2,1)S(1)}, u32[]{:S(2)}, u32[]{:S(2)}) async-start(bf16[64,80,128]{2,1,0:T(8,128)(2,1)} %get-tuple-element.15), calls=%async_computation.1 | async-start | bytes 2621440 | tf_op jit(solution)/shard_map/all_to_all | solution.py:458

commit v4 on v3

--- a/solution.py
+++ b/solution.py
@@ -7,6 +7,7 @@
 
 N_EL, N_FACE, N_PART, C_MAX = 16, 4, 64, 8
 N_JOB = C_MAX * N_FACE
+N_FIRST = 8
 R, N = 32, 320
 MIB = 2**20
 BF16, F32 = jnp.bfloat16, jnp.float32
@@ -81,8 +82,8 @@
 
 def early_kernel(
     refs, colour, listed, adj, rhs, upper, fj_own, fj_other,
-    send_out, local_out, base_out, adj_out, table,
-    order, send, local, up_buf, buf, up_sem, sem,
+    send_out, local_out, base_out, adj_out, table, first_out,
+    order, send, local, up_buf, buf, up_sem, sem, first_sem,
 ):
     count = order_by_colour(colour, order)
 
@@ -134,8 +135,19 @@
     near_jobs = list_faces(1, False, near, jnp.int32(0))
     close(far, jobs)
     close(near, near_jobs)
-    for k, number in enumerate((count, own_jobs, jobs, near_jobs)):
+    ready = jnp.minimum(lax.div(own_jobs, 4), N_FIRST // 4) * 4
+    for k, number in enumerate((count, own_jobs, jobs, near_jobs, ready)):
         table[k] = number
+
+    def first_copy(j):
+        block = table[JOB_BLOCK + j]
+        source = upper.at[lax.div(block, 2), lax.rem(block, 2)]
+        return pltpu.make_async_copy(source, first_out.at[j], first_sem)
+
+    @pl.loop(0, ready)
+    def _(j):
+        first_copy(j).start()
+
     for s in range(C_MAX):
         table[ELEM + s] = order[s]
 
@@ -168,6 +180,10 @@
     send_out[...] = send[:N_PART]
     local_out[...] = local[:N_EL]
 
+    @pl.loop(0, ready)
+    def _(j):
+        first_copy(j).wait()
+
 
 def arrive(jobs, buf, sem, g):
     left = jobs - 4 * g
@@ -207,7 +223,7 @@
 
 
 def sweep_kernel(
-    table_in, recv, base, upper, upper_other, dinv, fj_own, fj_other, new_in, send_in,
+    table_in, first, recv, base, upper, upper_other, dinv, fj_own, fj_other, new_in, send_in,
     new_out, send_out,
     table, start, total, new, row, up_buf, dinv_buf, fj_buf, up_sem, dinv_sem, fj_sem, base_sem, out_sem,
 ):
@@ -216,21 +232,21 @@
     table_copy.start()
     total[...] = jnp.zeros_like(total)
     table_copy.wait()
-    count, own_jobs, jobs = table[0], table[1], table[2]
+    count, own_jobs, jobs, ready = table[0], table[1], table[2], table[4]
     groups = lax.div(jobs + 3, 4)
 
-    def fetch(own, other, buf, sem):
+    def fetch(start_at, own, other, buf, sem):
         def copies(first, last, source):
             @pl.loop(first, last)
             def _(j):
                 block = source.at[table[JOB_BLOCK + j]]
                 pltpu.make_async_copy(block, buf.at[j], sem.at[lax.div(j, 4)]).start()
 
-        copies(0, own_jobs, own)
+        copies(start_at, own_jobs, own)
         copies(own_jobs, jobs, other)
 
     base_copy = pltpu.make_async_copy(base, start, base_sem)
-    fetch(upper, upper_other, up_buf, up_sem)
+    fetch(ready, upper, upper_other, up_buf, up_sem)
     base_copy.start()
     for part in range(2):
 
@@ -240,20 +256,22 @@
                 block = dinv.at[table[ELEM + s]]
                 pltpu.make_async_copy(block, dinv_buf.at[s], dinv_sem.at[part]).start()
 
-    fetch(fj_own, fj_other, fj_buf, fj_sem)
-
-    def in_groups(buf, sem, body):
-        @pl.loop(0, groups)
-        def _(g):
-            arrive(jobs, buf, sem, g)
-            body([4 * g + k for k in range(4)])
-
-    def push(js):
-        products = [dot(unpack(recv[table[JOB_AT + j]]), up_buf[j]) for j in js]
+    fetch(0, fj_own, fj_other, fj_buf, fj_sem)
+
+    def push(js, blocks):
+        products = [dot(unpack(recv[table[JOB_AT + j]]), blocks[j]) for j in js]
         for j, product in zip(js, products):
             total[table[JOB_S + j]] += product
 
-    in_groups(up_buf, up_sem, push)
+    @pl.loop(0, lax.div(ready, 4))
+    def _(g):
+        push([4 * g + k for k in range(4)], first)
+
+    @pl.loop(lax.div(ready, 4), groups)
+    def _(g):
+        arrive(jobs, up_buf, up_sem, g)
+        push([4 * g + k for k in range(4)], up_buf)
+
     base_copy.wait()
     def solve(slots):
         reduced = [(start[s] - total[s]).astype(BF16) for s in slots]
@@ -353,22 +371,19 @@
             out[i] = pack(rhs[i] - local[i] - dot(new[i], djac_buf[i]))
 
 
-def return_kernel(table_in, base, recv, out, table, base_buf, total, out_buf, in_sem, out_sem):
-    table_copy = pltpu.make_async_copy(table_in, table, in_sem.at[0])
-    base_copy = pltpu.make_async_copy(base, base_buf, in_sem.at[1])
+def return_kernel(table_in, base, recv, out, table, total, out_buf, in_sem, out_sem):
+    table_copy = pltpu.make_async_copy(table_in, table, in_sem)
     table_copy.start()
-    base_copy.start()
-    total[...] = jnp.zeros_like(total)
+    total[...] = base[...]
     table_copy.wait()
 
     @pl.loop(0, N_PART, unroll=8)
     def _(q):
-        total[table[LIST + q]] += recv[q].astype(F32)
-
-    base_copy.wait()
+        total[table[LIST + q]] -= recv[q].astype(F32)
+
     for g in range(4):
         for i in range(4 * g, 4 * g + 4):
-            out_buf[i] = unpack(base_buf[i] - total[i])
+            out_buf[i] = unpack(total[i])
         part = pl.ds(4 * g, 4)
         pltpu.make_async_copy(out_buf.at[part], out.at[part], out_sem).start()
     pltpu.make_async_copy(out_buf, out, out_sem).wait()
@@ -403,8 +418,7 @@
     DMA((2,)), DMA,
 ]
 RETURN_SCRATCH = [
-    pltpu.SMEM((TABLE,), jnp.int32),
-    pltpu.VMEM((N_EL, 80, 128), F32), pltpu.VMEM((N_EL, 80, 128), F32), pltpu.VMEM(LOCAL, F32), DMA((2,)), DMA,
+    pltpu.SMEM((TABLE,), jnp.int32), pltpu.VMEM((N_EL, 80, 128), F32), pltpu.VMEM(LOCAL, F32), DMA, DMA,
 ]
 SWEEP_SCRATCH = [
     pltpu.SMEM((TABLE,), jnp.int32),
@@ -429,14 +443,14 @@
     )(listed, adj)
     incoming = lax.all_to_all(outgoing, "dom", split_axis=0, concat_axis=0, tiled=True)
 
-    sent, local, base_own, kept, table = call(
+    sent, local, base_own, kept, table, first = call(
         early_kernel,
         (hbm(ROWS), hbm(LOCAL, F32), hbm((C_MAX, R, N), F32), hbm(LOCAL),
-         jax.ShapeDtypeStruct((TABLE,), jnp.int32)),
-        [SMEM, SMEM, SMEM, VMEM, VMEM, HBM, HBM, HBM], (VMEM, VMEM, VMEM, VMEM, SMEM),
+         jax.ShapeDtypeStruct((TABLE,), jnp.int32), jax.ShapeDtypeStruct((N_FIRST, N, N), BF16)),
+        [SMEM, SMEM, SMEM, VMEM, VMEM, HBM, HBM, HBM], (VMEM, VMEM, VMEM, VMEM, SMEM, VMEM),
         [ORDER, pltpu.VMEM((N_PART + 1, 80, 128), BF16), pltpu.VMEM((N_EL + 1, R, N), F32),
          pltpu.VMEM((C_MAX, 2, N, N), BF16), pltpu.VMEM((N_EL, N_FACE, N, N), BF16),
-         DMA((C_MAX,)), DMA((N_EL,))],
+         DMA((C_MAX,)), DMA((N_EL,)), DMA],
         36,
     )(refs, colour, listed, adj, rhs, pin(upper), fj, fj_other)
 
@@ -449,25 +463,25 @@
 
     new, outbound = call(
         sweep_kernel, (hbm(LOCAL), hbm(ROWS)),
-        [VMEM, VMEM, HBM, HBM, HBM, HBM, HBM, HBM, HBM, HBM], (HBM, HBM),
+        [VMEM, VMEM, VMEM, HBM, HBM, HBM, HBM, HBM, HBM, HBM, HBM], (HBM, HBM),
         SWEEP_SCRATCH,
-        32, {8: 0, 9: 1},
-    )(table, incoming, pin(base), pin(upper.reshape(blocks)), pin(upper_other.reshape(blocks)),
+        32, {9: 0, 10: 1},
+    )(table, first, incoming, pin(base), pin(upper.reshape(blocks)), pin(upper_other.reshape(blocks)),
       pin(diag_inv), pin(face_jac.reshape(blocks)), pin(face_jac_other.reshape(blocks)), pin(kept),
       pin(sent))
     inbound = lax.all_to_all(outbound, "dom", split_axis=0, concat_axis=0, tiled=True)
 
     own = call(
-        diagonal_kernel, hbm((N_EL, 80, 128), F32), [SMEM, SMEM, VMEM, VMEM, HBM, HBM, HBM, HBM], VMEM,
+        diagonal_kernel, jax.ShapeDtypeStruct((N_EL, 80, 128), F32), [SMEM, SMEM, VMEM, VMEM, HBM, HBM, HBM, HBM], VMEM,
         [ORDER, pltpu.VMEM((N_EL + 1, R, N), F32), pltpu.VMEM((N_EL, N, N), BF16),
          pltpu.VMEM((C_MAX, N_FACE, N, N), BF16), DMA, DMA((4,)), DMA((C_MAX,))],
         20,
     )(refs, colour, rhs, pin(new), pin(local), pin(diag_jac), fj, fj_other)
 
     residual = call(
-        return_kernel, hbm(LOCAL, F32), [VMEM, HBM, VMEM], HBM, RETURN_SCRATCH,
+        return_kernel, hbm(LOCAL, F32), [VMEM, VMEM, VMEM], HBM, RETURN_SCRATCH,
         8,
-    )(table, pin(own), inbound)
+    )(table, own, inbound)
     return new, residual
 
 

time: 70.4 us -> 69.4 us (0.986)
  Pallas kernels: 27.1 us -> 24.7 us
  waiting for transfers between devices: 24.4 us -> 25.2 us
    pallas_call x3, Pallas kernels: 13.3 us -> 10.5 us  [the longest x1 4.9 us: on_device(): call(diagonal_kernel, jax.ShapeDtypeStruct((N_EL, 80, 128), F32), [SMEM,...]
    all_to_all x1, waiting for transfers between devices: 14.3 us -> 15.5 us  [on_device(): lax.all_to_all(outbound, 'dom', split_axis=0, concat_axis=0, tiled=True)]
  transfers between devices with their start and end apart: 4 -> 4, of which waited for: 3 -> 3; matrix products, arithmetic and copies ran while one was open for 0% -> 0% of each run, Pallas kernels for 29% -> 28%
where the time goes in v4:
time: 69.4 us; the launch traced here: 68.8 us
  waiting for transfers between devices  25.2 us (36%)
  Pallas kernels  24.7 us (36%)
  starting transfers between devices  18.3 us (26%)
  between operations  0.7 us (1%)
    all_to_all x1, waiting for transfers between devices, on_device(): lax.all_to_all(outbound, 'dom', split_axis=0, concat_axis=0, tiled=True)  15.5 us
    all_to_all x1, starting transfers between devices, on_device(): lax.all_to_all(outgoing, 'dom', split_axis=0, concat_axis=0, tiled=True)  11.5 us
    pallas_call x1, Pallas kernels, on_device(): call(early_kernel, (hbm(ROWS), hbm(LOCAL, F32), hbm((C_MAX, R, N), F32),...  9.49 us
    all_to_all x1, waiting for transfers between devices, on_device(): lax.all_to_all(outgoing, 'dom', split_axis=0, concat_axis=0, tiled=True)  9.44 us
    all_to_all x1, starting transfers between devices, on_device(): lax.all_to_all(outbound, 'dom', split_axis=0, concat_axis=0, tiled=True)  6.16 us
    pallas_call x1, Pallas kernels, on_device(): call(diagonal_kernel, jax.ShapeDtypeStruct((N_EL, 80, 128), F32), [SMEM,...  4.9 us
    pallas_call x1, Pallas kernels, on_device(): call(sweep_kernel, (hbm(LOCAL), hbm(ROWS)), [VMEM, VMEM, VMEM, HBM, HBM,...  3.75 us
    pallas_call x1, Pallas kernels, on_device(): call(near_kernel, hbm((C_MAX, R, N), F32), [SMEM, HBM, HBM, HBM], HBM, [p...  2.49 us
  transfers between devices with their start and end apart: 4, of which 3 were waited for; matrix products, arithmetic and copies ran while one was open for 0% of the time, Pallas kernels for 28%

profile of v4, /device:TPU:0, one launch (start us, length us, event | category | flops | bytes accessed | tf_op | source)
XLA Modules:
  0.0 68.8 jit_solution(696087946252105527)
XLA Ops:
  0.6 0.1 collective-permute-start
  0.7 0.5 collective-permute-start.1
  1.2 2.2 %pack_kernel.1 = bf16[64,80,128]{2,1,0:T(8,128)(2,1)} custom-call(s32[64]{0:T(128)} %bitcast.10, bf16[16,32,320]{2,1,0:T(8,128)(2,1)} %adj.5), custom_call_target="tpu_custom_call" | custom-call | tf_op jit(solution)/shard_map/pack_kernel/pallas_call | solution.py:440
  3.4 11.5 %all-to-all-start = ((bf16[64,80,128]{2,1,0:T(8,128)(2,1)}), bf16[64,80,128]{2,1,0:T(8,128)(2,1)S(1)}, u32[]{:S(2)}, u32[]{:S(2)}) async-start(bf16[64,80,128]{2,1,0:T(8,128)(2,1)} %pack_kernel.1), calls=%async_computation | async-start | bytes 2621440 | tf_op jit(solution)/shard_map/all_to_all | solution.py:444
  15.0 0.0 collective-permute-done.fj_other
  15.0 9.5 %early_kernel.1 = (bf16[64,80,128]{2,1,0:T(8,128)(2,1)}, f32[16,32,320]{2,1,0:T(8,128)}, f32[8,32,320]{2,1,0:T(8,128)}, bf16[16,32,320]{2,1,0:T(8,128)(2,1)}, s3...) custom-call(s32[4,16]{1,0:T(4,128)} %bitcast.8, s32[16]{0:T(128)} %colour.3, s32[64]{0:T(128)} %bitcast.11, ...), custom_call_target="tpu_custom_call" | custom-call | tf_op jit(solution)/shard_map/early_kernel/pallas_call | solution.py:446
  24.5 0.2 collective-permute-done.1
  24.7 2.5 %near_kernel.1.base = f32[8,32,320]{2,1,0:T(8,128)} custom-call(s32[288]{0:T(512)S(1)} %get-tuple-element.10.table.table_in, bf16[16,32,320]{2,1,0:T(8,128)(2,1)} %adj.5, f32[8,32,320]{2,1,0:T(8,128)} %get-tuple-element.12.base, bf16[32,320,320]{2,1,0:T(8,128)(2,1)} %bitcast.2.upper_other), custom_call_target="tpu_custom_call" | custom-call | tf_op jit(solution)/shard_map/near_kernel/pallas_call | solution.py:457
  27.2 9.4 %all-to-all-done.recv = bf16[64,80,128]{2,1,0:T(8,128)(2,1)S(1)} async-done(((bf16[64,80,128]{2,1,0:T(8,128)(2,1)}), bf16[64,80,128]{2,1,0:T(8,128)(2,1)S(1)}, u32[]{:S(2)}, u32[]{:S(2)}) %all-to-all-start) | async-done | bytes 1310752 | tf_op jit(solution)/shard_map/all_to_all | solution.py:444
  36.7 3.7 %sweep_kernel.1 = (bf16[16,32,320]{2,1,0:T(8,128)(2,1)}, bf16[64,80,128]{2,1,0:T(8,128)(2,1)}) custom-call(s32[288]{0:T(512)S(1)} %get-tuple-element.10.table.table_in, bf16[8,320,320]{2,1,0:T(8,128)(2,1)S(1)} %get-tuple-element.11.first, bf16[64,80,128]{2,1,0:T(8,128)(2,1)S(1)} %all-to-all-done.recv, ...), custom_call_target="tpu_custom_call", output_to_operand_aliasing={{0}: (9, {}), {1}: (10, {})} | custom-call | tf_op jit(solution)/shard_map/sweep_kernel/pallas_call | solution.py:464
  40.4 6.2 %all-to-all-start.1 = ((bf16[64,80,128]{2,1,0:T(8,128)(2,1)}), bf16[64,80,128]{2,1,0:T(8,128)(2,1)S(1)}, u32[]{:S(2)}, u32[]{:S(2)}) async-start(bf16[64,80,128]{2,1,0:T(8,128)(2,1)} %get-tuple-element.17), calls=%async_computation.1 | async-start | bytes 2621440 | tf_op jit(solution)/shard_map/all_to_all | solution.py:472
  46.6 4.9 %diagonal_kernel.1.base = f32[16,80,128]{2,1,0:T(8,128)S(1)} custom-call(s32[4,16]{1,0:T(4,128)} %bitcast.9, s32[16]{0:T(128)} %colour.3, f32[16,32,320]{2,1,0:T(8,128)} %rhs.3, bf16[16,32,320]{2,1,0:T(8,128)(2,1)} %get-tuple-element.8.new, f32[16,32,320]{2,1,0:T(8,128)} %get-tuple-element.16.local_in, bf16[16,320,320]{2,1,0:T(8,128)(2,1)} %djac.1, ...), custom_call_target="tpu_custom_call" | custom-call | tf_op jit(solution)/shard_map/diagonal_kernel/pallas_call | solution.py:474
  51.5 15.5 %all-to-all-done.1.recv = bf16[64,80,128]{2,1,0:T(8,128)(2,1)S(1)} async-done(((bf16[64,80,128]{2,1,0:T(8,128)(2,1)}), bf16[64,80,128]{2,1,0:T(8,128)(2,1)S(1)}, u32[]{:S(2)}, u32[]{:S(2)}) %all-to-all-start.1) | async-done | bytes 1310752 | tf_op jit(solution)/shard_map/all_to_all | solution.py:472
  67.0 1.9 %return_kernel.1 = f32[16,32,320]{2,1,0:T(8,128)} custom-call(s32[288]{0:T(512)S(1)} %get-tuple-element.10.table.table_in, f32[16,80,128]{2,1,0:T(8,128)S(1)} %diagonal_kernel.1.base, bf16[64,80,128]{2,1,0:T(8,128)(2,1)S(1)} %all-to-all-done.1.recv), custom_call_target="tpu_custom_call" | custom-call | tf_op jit(solution)/shard_map/return_kernel/pallas_call | solution.py:481
Async XLA Ops:
  0.6 14.3 %collective-permute-start = (bf16[16,2,320,320]{3,2,1,0:T(8,128)(2,1)}, bf16[16,2,320,320]{3,2,1,0:T(8,128)(2,1)}, u32[]{:S(2)}, u32[]{:S(2)}) collective-permute-start(bf16[16,2,320,320]{3,2,1,0:T(8,128)(2,1)} %fj_own.3), channel_id=1, source_target_pairs={{0,1},{1,0},{2,3},{3,2},{4,5},{5,4},{6,7},{7,6},{8,9},{9,8},{10,11... | collective-permute-start | bytes 19660808 | tf_op jit(solution)/shard_map/ppermute | solution.py:436
  0.7 24.0 %collective-permute-start.1 = (bf16[16,2,320,320]{3,2,1,0:T(8,128)(2,1)}, bf16[16,2,320,320]{3,2,1,0:T(8,128)(2,1)}, u32[]{:S(2)}, u32[]{:S(2)}) collective-permute-start(bf16[16,2,320,320]{3,2,1,0:T(8,128)(2,1)} %upper.1), channel_id=1, source_target_pairs={{0,1},{1,0},{2,3},{3,2},{4,5},{5,4},{6,7},{7,6},{8,9},{9,8},{10,11... | collective-permute-start | bytes 19660808 | tf_op jit(solution)/shard_map/ppermute | solution.py:437
  3.4 33.2 %all-to-all-start = ((bf16[64,80,128]{2,1,0:T(8,128)(2,1)}), bf16[64,80,128]{2,1,0:T(8,128)(2,1)S(1)}, u32[]{:S(2)}, u32[]{:S(2)}) async-start(bf16[64,80,128]{2,1,0:T(8,128)(2,1)} %pack_kernel.1), calls=%async_computation | async-start | bytes 2621440 | tf_op jit(solution)/shard_map/all_to_all | solution.py:444
  40.4 26.6 %all-to-all-start.1 = ((bf16[64,80,128]{2,1,0:T(8,128)(2,1)}), bf16[64,80,128]{2,1,0:T(8,128)(2,1)S(1)}, u32[]{:S(2)}, u32[]{:S(2)}) async-start(bf16[64,80,128]{2,1,0:T(8,128)(2,1)} %get-tuple-element.17), calls=%async_computation.1 | async-start | bytes 2621440 | tf_op jit(solution)/shard_map/all_to_all | solution.py:472

commit v5 on v4

--- a/solution.py
+++ b/solution.py
@@ -135,7 +135,7 @@
     near_jobs = list_faces(1, False, near, jnp.int32(0))
     close(far, jobs)
     close(near, near_jobs)
-    ready = jnp.minimum(lax.div(own_jobs, 4), N_FIRST // 4) * 4
+    ready = jnp.minimum(own_jobs, N_FIRST)
     for k, number in enumerate((count, own_jobs, jobs, near_jobs, ready)):
         table[k] = number
 
@@ -194,7 +194,10 @@
             landed(buf.at[pl.ds(4 * g, n)], sem.at[g])
 
 
-def near_kernel(table, adj, base, upper_other, out, own, total, buf, in_sem, sem, out_sem):
+def near_kernel(table_in, adj, base, upper_other, out, table, own, total, buf, in_sem, sem, out_sem):
+    table_copy = pltpu.make_async_copy(table_in, table, out_sem)
+    table_copy.start()
+    table_copy.wait()
     jobs = table[3]
     adj_copy = pltpu.make_async_copy(adj, own, in_sem.at[0])
     base_copy = pltpu.make_async_copy(base, total.at[pl.ds(0, C_MAX)], in_sem.at[1])
@@ -240,7 +243,8 @@
             @pl.loop(first, last)
             def _(j):
                 block = source.at[table[JOB_BLOCK + j]]
-                pltpu.make_async_copy(block, buf.at[j], sem.at[lax.div(j, 4)]).start()
+                at = j - start_at
+                pltpu.make_async_copy(block, buf.at[at], sem.at[lax.div(at, 4)]).start()
 
         copies(start_at, own_jobs, own)
         copies(own_jobs, jobs, other)
@@ -258,19 +262,22 @@
 
     fetch(0, fj_own, fj_other, fj_buf, fj_sem)
 
-    def push(js, blocks):
-        products = [dot(unpack(recv[table[JOB_AT + j]]), blocks[j]) for j in js]
-        for j, product in zip(js, products):
-            total[table[JOB_S + j]] += product
-
-    @pl.loop(0, lax.div(ready, 4))
+    def push(js, rows, blocks):
+        products = [dot(unpack(recv[table[JOB_AT + j]]), block) for j, block in zip(js, blocks)]
+        for at, product in zip(rows, products):
+            total[at] += product
+
+    @pl.loop(0, lax.div(ready + 3, 4))
     def _(g):
-        push([4 * g + k for k in range(4)], first)
-
-    @pl.loop(lax.div(ready, 4), groups)
+        js = [4 * g + k for k in range(4)]
+        rows = [jnp.where(j < ready, table[JOB_S + j], C_MAX) for j in js]
+        push(js, rows, [first[j] for j in js])
+
+    @pl.loop(0, lax.div(jobs - ready + 3, 4))
     def _(g):
-        arrive(jobs, up_buf, up_sem, g)
-        push([4 * g + k for k in range(4)], up_buf)
+        arrive(jobs - ready, up_buf, up_sem, g)
+        js = [ready + 4 * g + k for k in range(4)]
+        push(js, [table[JOB_S + j] for j in js], [up_buf[4 * g + k] for k in range(4)])
 
     base_copy.wait()
     def solve(slots):
@@ -455,8 +462,8 @@
     )(refs, colour, listed, adj, rhs, pin(upper), fj, fj_other)
 
     base = call(
-        near_kernel, hbm((C_MAX, R, N), F32), [SMEM, HBM, HBM, HBM], HBM,
-        [pltpu.VMEM(LOCAL, BF16), pltpu.VMEM((C_MAX + 1, R, N), F32),
+        near_kernel, hbm((C_MAX, R, N), F32), [VMEM, HBM, HBM, HBM], HBM,
+        [pltpu.SMEM((TABLE,), jnp.int32), pltpu.VMEM(LOCAL, BF16), pltpu.VMEM((C_MAX + 1, R, N), F32),
          pltpu.VMEM((2 * C_MAX, N, N), BF16), DMA((2,)), DMA((C_MAX // 2,)), DMA],
         8,
     )(table, adj, pin(base_own), pin(upper_other.reshape(blocks)))

time: 69.4 us -> 70.1 us (1.010)
  Pallas kernels: 24.7 us -> 25.8 us
  transfers between devices with their start and end apart: 4 -> 4, of which waited for: 3 -> 3; matrix products, arithmetic and copies ran while one was open for 0% -> 0% of each run, Pallas kernels for 28% -> 29%
where the time goes in v5:
time: 70.1 us; the launch traced here: 69.3 us
  Pallas kernels  25.8 us (37%)
  waiting for transfers between devices  24.6 us (35%)
  starting transfers between devices  18.3 us (26%)
    all_to_all x1, waiting for transfers between devices, on_device(): lax.all_to_all(outbound, 'dom', split_axis=0, concat_axis=0, tiled=True)  15.2 us
    all_to_all x1, starting transfers between devices, on_device(): lax.all_to_all(outgoing, 'dom', split_axis=0, concat_axis=0, tiled=True)  11.5 us
    pallas_call x1, Pallas kernels, on_device(): call(early_kernel, (hbm(ROWS), hbm(LOCAL, F32), hbm((C_MAX, R, N), F32),...  9.34 us
    all_to_all x1, waiting for transfers between devices, on_device(): lax.all_to_all(outgoing, 'dom', split_axis=0, concat_axis=0, tiled=True)  8.93 us
    all_to_all x1, starting transfers between devices, on_device(): lax.all_to_all(outbound, 'dom', split_axis=0, concat_axis=0, tiled=True)  6.21 us
    pallas_call x1, Pallas kernels, on_device(): call(diagonal_kernel, jax.ShapeDtypeStruct((N_EL, 80, 128), F32), [SMEM,...  5.2 us
    pallas_call x1, Pallas kernels, on_device(): call(sweep_kernel, (hbm(LOCAL), hbm(ROWS)), [VMEM, VMEM, VMEM, HBM, HBM,...  4.16 us
    pallas_call x1, Pallas kernels, on_device(): call(near_kernel, hbm((C_MAX, R, N), F32), [VMEM, HBM, HBM, HBM], HBM, [p...  3.01 us
  transfers between devices with their start and end apart: 4, of which 3 were waited for; matrix products, arithmetic and copies ran while one was open for 0% of the time, Pallas kernels for 29%

profile of v5, /device:TPU:0, one launch (start us, length us, event | category | flops | bytes accessed | tf_op | source)
XLA Modules:
  0.0 69.3 jit_solution(16527122805820079096)
XLA Ops:
  0.6 0.1 collective-permute-start
  0.7 0.5 collective-permute-start.1
  1.2 2.2 %pack_kernel.1 = bf16[64,80,128]{2,1,0:T(8,128)(2,1)} custom-call(s32[64]{0:T(128)} %bitcast.10, bf16[16,32,320]{2,1,0:T(8,128)(2,1)} %adj.5), custom_call_target="tpu_custom_call" | custom-call | tf_op jit(solution)/shard_map/pack_kernel/pallas_call | solution.py:447
  3.4 11.5 %all-to-all-start = ((bf16[64,80,128]{2,1,0:T(8,128)(2,1)}), bf16[64,80,128]{2,1,0:T(8,128)(2,1)S(1)}, u32[]{:S(2)}, u32[]{:S(2)}) async-start(bf16[64,80,128]{2,1,0:T(8,128)(2,1)} %pack_kernel.1), calls=%async_computation | async-start | bytes 2621440 | tf_op jit(solution)/shard_map/all_to_all | solution.py:451
  15.0 0.0 collective-permute-done.fj_other
  15.0 9.3 %early_kernel.1 = (bf16[64,80,128]{2,1,0:T(8,128)(2,1)}, f32[16,32,320]{2,1,0:T(8,128)}, f32[8,32,320]{2,1,0:T(8,128)}, bf16[16,32,320]{2,1,0:T(8,128)(2,1)}, s3...) custom-call(s32[4,16]{1,0:T(4,128)} %bitcast.8, s32[16]{0:T(128)} %colour.3, s32[64]{0:T(128)} %bitcast.11, ...), custom_call_target="tpu_custom_call" | custom-call | tf_op jit(solution)/shard_map/early_kernel/pallas_call | solution.py:453
  24.3 0.4 collective-permute-done.1
  24.7 3.0 %near_kernel.1.base = f32[8,32,320]{2,1,0:T(8,128)} custom-call(s32[288]{0:T(512)S(1)} %get-tuple-element.10.table_in, bf16[16,32,320]{2,1,0:T(8,128)(2,1)} %adj.5, f32[8,32,320]{2,1,0:T(8,128)} %get-tuple-element.12.base, bf16[32,320,320]{2,1,0:T(8,128)(2,1)} %bitcast.2.upper_other), custom_call_target="tpu_custom_call" | custom-call | tf_op jit(solution)/shard_map/near_kernel/pallas_call | solution.py:464
  27.7 8.9 %all-to-all-done.recv = bf16[64,80,128]{2,1,0:T(8,128)(2,1)S(1)} async-done(((bf16[64,80,128]{2,1,0:T(8,128)(2,1)}), bf16[64,80,128]{2,1,0:T(8,128)(2,1)S(1)}, u32[]{:S(2)}, u32[]{:S(2)}) %all-to-all-start) | async-done | bytes 1310752 | tf_op jit(solution)/shard_map/all_to_all | solution.py:451
  36.7 4.2 %sweep_kernel.1 = (bf16[16,32,320]{2,1,0:T(8,128)(2,1)}, bf16[64,80,128]{2,1,0:T(8,128)(2,1)}) custom-call(s32[288]{0:T(512)S(1)} %get-tuple-element.10.table_in, bf16[8,320,320]{2,1,0:T(8,128)(2,1)S(1)} %get-tuple-element.11.first, bf16[64,80,128]{2,1,0:T(8,128)(2,1)S(1)} %all-to-all-done.recv, ...), custom_call_target="tpu_custom_call", output_to_operand_aliasing={{0}: (9, {}), {1}: (10, {})} | custom-call | tf_op jit(solution)/shard_map/sweep_kernel/pallas_call | solution.py:471
  40.8 6.2 %all-to-all-start.1 = ((bf16[64,80,128]{2,1,0:T(8,128)(2,1)}), bf16[64,80,128]{2,1,0:T(8,128)(2,1)S(1)}, u32[]{:S(2)}, u32[]{:S(2)}) async-start(bf16[64,80,128]{2,1,0:T(8,128)(2,1)} %get-tuple-element.17), calls=%async_computation.1 | async-start | bytes 2621440 | tf_op jit(solution)/shard_map/all_to_all | solution.py:479
  47.0 5.2 %diagonal_kernel.1.base = f32[16,80,128]{2,1,0:T(8,128)S(1)} custom-call(s32[4,16]{1,0:T(4,128)} %bitcast.9, s32[16]{0:T(128)} %colour.3, f32[16,32,320]{2,1,0:T(8,128)} %rhs.3, bf16[16,32,320]{2,1,0:T(8,128)(2,1)} %get-tuple-element.8.new, f32[16,32,320]{2,1,0:T(8,128)} %get-tuple-element.16.local_in, bf16[16,320,320]{2,1,0:T(8,128)(2,1)} %djac.1, ...), custom_call_target="tpu_custom_call" | custom-call | tf_op jit(solution)/shard_map/diagonal_kernel/pallas_call | solution.py:481
  52.3 15.2 %all-to-all-done.1.recv = bf16[64,80,128]{2,1,0:T(8,128)(2,1)S(1)} async-done(((bf16[64,80,128]{2,1,0:T(8,128)(2,1)}), bf16[64,80,128]{2,1,0:T(8,128)(2,1)S(1)}, u32[]{:S(2)}, u32[]{:S(2)}) %all-to-all-start.1) | async-done | bytes 1310752 | tf_op jit(solution)/shard_map/all_to_all | solution.py:479
  67.5 1.9 %return_kernel.1 = f32[16,32,320]{2,1,0:T(8,128)} custom-call(s32[288]{0:T(512)S(1)} %get-tuple-element.10.table_in, f32[16,80,128]{2,1,0:T(8,128)S(1)} %diagonal_kernel.1.base, bf16[64,80,128]{2,1,0:T(8,128)(2,1)S(1)} %all-to-all-done.1.recv), custom_call_target="tpu_custom_call" | custom-call | tf_op jit(solution)/shard_map/return_kernel/pallas_call | solution.py:488
Async XLA Ops:
  0.6 14.3 %collective-permute-start = (bf16[16,2,320,320]{3,2,1,0:T(8,128)(2,1)}, bf16[16,2,320,320]{3,2,1,0:T(8,128)(2,1)}, u32[]{:S(2)}, u32[]{:S(2)}) collective-permute-start(bf16[16,2,320,320]{3,2,1,0:T(8,128)(2,1)} %fj_own.3), channel_id=1, source_target_pairs={{0,1},{1,0},{2,3},{3,2},{4,5},{5,4},{6,7},{7,6},{8,9},{9,8},{10,11... | collective-permute-start | bytes 19660808 | tf_op jit(solution)/shard_map/ppermute | solution.py:443
  0.7 24.0 %collective-permute-start.1 = (bf16[16,2,320,320]{3,2,1,0:T(8,128)(2,1)}, bf16[16,2,320,320]{3,2,1,0:T(8,128)(2,1)}, u32[]{:S(2)}, u32[]{:S(2)}) collective-permute-start(bf16[16,2,320,320]{3,2,1,0:T(8,128)(2,1)} %upper.1), channel_id=1, source_target_pairs={{0,1},{1,0},{2,3},{3,2},{4,5},{5,4},{6,7},{7,6},{8,9},{9,8},{10,11... | collective-permute-start | bytes 19660808 | tf_op jit(solution)/shard_map/ppermute | solution.py:444
  3.4 33.2 %all-to-all-start = ((bf16[64,80,128]{2,1,0:T(8,128)(2,1)}), bf16[64,80,128]{2,1,0:T(8,128)(2,1)S(1)}, u32[]{:S(2)}, u32[]{:S(2)}) async-start(bf16[64,80,128]{2,1,0:T(8,128)(2,1)} %pack_kernel.1), calls=%async_computation | async-start | bytes 2621440 | tf_op jit(solution)/shard_map/all_to_all | solution.py:451
  40.8 26.7 %all-to-all-start.1 = ((bf16[64,80,128]{2,1,0:T(8,128)(2,1)}), bf16[64,80,128]{2,1,0:T(8,128)(2,1)S(1)}, u32[]{:S(2)}, u32[]{:S(2)}) async-start(bf16[64,80,128]{2,1,0:T(8,128)(2,1)} %get-tuple-element.17), calls=%async_computation.1 | async-start | bytes 2621440 | tf_op jit(solution)/shard_map/all_to_all | solution.py:479
